TPU v7x, 256 devices: a whole 4x4x8 slice. The times are simulated.
256 devices in a mesh: queue: 16 (over y_hi, x, core), space: 16 (over y_lo, z).
Axes of the slice: x: 4, y: 4 (y_hi: 2, y_lo: 2; y = y_hi * 2 + y_lo), z: 8, core: 2. Of those that a mesh axis runs over, the one named last changes fastest.
Arguments:
- latents: float32 [16, 4, 16, 48, 16], P('queue', None, None, 'space'), as said below
- fresh_noise: float32 [4, 16, 48, 16], P(None, None, 'space'), may hold values from -6 to 6
- timesteps: int32 [16], replicated, may hold values from 50 to 999, as said below
- queue_map: int32 [16], replicated, may hold values from 0 to 15, as said below
- conv_in_w: bfloat16 [3, 3, 4, 320], replicated, may hold values from -1 to 1
- time_w1: bfloat16 [320, 1280], replicated, may hold values from -0.3125 to 0.3125
- time_w2: bfloat16 [1280, 1280], replicated, may hold values from -0.15625 to 0.15625
- emb_w: bfloat16 [1280, 320], replicated, may hold values from -0.15625 to 0.15625
- conv1_w: bfloat16 [3, 3, 320, 320], replicated, may hold values from -0.109375 to 0.109375
- conv2_w: bfloat16 [3, 3, 320, 320], replicated, may hold values from -0.109375 to 0.109375
- qkv_w: bfloat16 [320, 960], replicated
- proj_w: bfloat16 [320, 320], replicated, may hold values from -0.3125 to 0.3125
- conv_out_w: bfloat16 [3, 3, 320, 4], replicated, may hold values from -0.109375 to 0.109375
Outputs:
- noise_pred: float32 [16, 4, 16, 48, 16], P('queue', None, None, 'space')
- next_queue: float32 [16, 4, 16, 48, 16], P('queue', None, None, 'space')
Inputs may be any that keep to these rules, and one draw needn't show every extreme that they name: `queue_map`: each queue position names a different frame group. timesteps[queue_map[p]] rises strictly with the queue position p. Noisy latents.
All inputs are finite; a program needn't handle non-finite values.
Results may differ from a plain program's by a relative error of at most 0.0095.
Values may be sent and summed in bfloat16 or wider, within the bound.
A program may use at most 64 MiB of HBM per device.

v0:
```python
import math

import jax
import jax.numpy as jnp
from jax import lax
from jax.sharding import PartitionSpec as P

GROUPS = 32
HEAD_DIM = 64
STEP = 50


NORM_EPS = 1e-05


def with_halo(cells, sides, width):
    for axis, dim in sides:
        count = lax.axis_size(axis)
        ends = count - 1
        head = lax.slice_in_dim(cells, 0, width, axis=dim)
        tail = lax.slice_in_dim(cells, cells.shape[dim] - width, cells.shape[dim], axis=dim)
        cells = jnp.concatenate(
            [
                lax.ppermute(tail, axis, [(i, (i + 1) % count) for i in range(ends)]),
                cells,
                lax.ppermute(head, axis, [((i + 1) % count, i) for i in range(ends)]),
            ],
            axis=dim,
        )
    return cells


def from_behind(block, axis, distance):
    devices = range(lax.axis_size(axis))
    route = [(i - distance, i) for i in devices if i - distance in devices]
    return lax.ppermute(block, axis, route)


def alpha_table():
    betas = jnp.linspace(0.00085**0.5, 0.012**0.5, 1000, dtype=jnp.float32) ** 2
    return jnp.cumprod(1.0 - betas)


def norm_stats(features):
    channels = features.shape[3]
    cell_count = (
        features.shape[0]
        * features.shape[1]
        * lax.axis_size("space")
        * features.shape[2]
        * (channels // GROUPS)
    )
    shaped = features.reshape(features.shape[:3] + (GROUPS, channels // GROUPS))
    centre = lax.psum(jnp.sum(shaped, axis=(0, 1, 2, 4)), "space") / cell_count
    spread = (
        lax.psum(jnp.sum((shaped - centre[:, None]) ** 2, axis=(0, 1, 2, 4)), "space") / cell_count
    )
    return (centre, lax.rsqrt(spread + NORM_EPS))


def apply_norm(features, stats):
    centre, inverse = stats
    shaped = features.reshape(features.shape[:3] + (GROUPS, features.shape[3] // GROUPS))
    return ((shaped - centre[:, None]) * inverse[:, None]).reshape(features.shape)


def convolve_rows(padded_rows, weight, row_count):
    padded = jnp.pad(padded_rows, ((0, 0), (0, 0), (1, 1), (0, 0)))
    frame_count = padded.shape[0]
    col_count = padded.shape[2] - 2
    in_ch = padded.shape[3]
    accum = jnp.zeros((frame_count * row_count * col_count, weight.shape[3]), jnp.float32)
    for row_tap in range(3):
        for col_tap in range(3):
            window = padded[:, row_tap : row_tap + row_count, col_tap : col_tap + col_count, :]
            accum = accum + jnp.dot(
                window.reshape(-1, in_ch),
                weight[row_tap, col_tap],
                preferred_element_type=jnp.float32,
            )
    return accum.reshape(frame_count, row_count, col_count, weight.shape[3])


def res_halo(features):
    return with_halo(features, (("space", 1),), 1)


def time_embedding(noise_level, time_w1, time_w2, emb_w):
    half_width = time_w1.shape[0] // 2
    frequency = jnp.exp(-math.log(10000.0) * jnp.arange(half_width, dtype=jnp.float32) / half_width)
    phases = noise_level.astype(jnp.float32) * frequency
    sinusoid = jnp.concatenate([jnp.cos(phases), jnp.sin(phases)])[None].astype(jnp.bfloat16)
    first_hidden = jax.nn.silu(
        jnp.dot(sinusoid, time_w1, preferred_element_type=jnp.float32)
    ).astype(jnp.bfloat16)
    second = jax.nn.silu(jnp.dot(first_hidden, time_w2, preferred_element_type=jnp.float32)).astype(
        jnp.bfloat16
    )
    return jnp.dot(second, emb_w, preferred_element_type=jnp.float32)[0]


def attend(attn_in, qkv_w, proj_w):
    frame_count, row_count, col_count, channels = attn_in.shape
    projected = jnp.dot(
        attn_in.reshape(-1, channels), qkv_w, preferred_element_type=jnp.float32
    ).astype(jnp.bfloat16)
    projected = projected.reshape(
        frame_count, row_count, col_count, 3, channels // HEAD_DIM, HEAD_DIM
    )
    queries = projected[:, :, :, 0]
    keys_all = projected[:, :, :, 1]
    values = projected[:, :, :, 2]
    scores = jnp.einsum(
        "fhwnd,ghwnd->hwnfg", queries, keys_all, preferred_element_type=jnp.float32
    ) * HEAD_DIM ** (-0.5)
    probs = jax.nn.softmax(scores, axis=-1).astype(jnp.bfloat16)
    attended = jnp.einsum(
        "hwnfg,ghwnd->fhwnd", probs, values, preferred_element_type=jnp.float32
    ).astype(jnp.bfloat16)
    attended = attended.reshape(-1, channels)
    return jnp.dot(attended, proj_w, preferred_element_type=jnp.float32).reshape(attn_in.shape)


def per_device(
    latents,
    fresh_noise,
    timesteps,
    queue_map,
    conv_in_w,
    time_w1,
    time_w2,
    emb_w,
    conv1_w,
    conv2_w,
    qkv_w,
    proj_w,
    conv_out_w,
):
    latent = latents[0]
    row_count = latent.shape[2]
    position = lax.axis_index("queue")
    noise_level = timesteps[queue_map[position]]
    alphas = alpha_table()
    latent_rows = with_halo(latent.astype(jnp.bfloat16), (("space", 2),), 1)
    stream = convolve_rows(jnp.transpose(latent_rows, (1, 2, 3, 0)), conv_in_w, row_count)
    time_bias = time_embedding(noise_level, time_w1, time_w2, emb_w)
    normed1 = jax.nn.silu(apply_norm(stream, norm_stats(stream))).astype(jnp.bfloat16)
    hidden1 = convolve_rows(res_halo(normed1), conv1_w, row_count) + time_bias
    normed2 = jax.nn.silu(apply_norm(hidden1, norm_stats(hidden1))).astype(jnp.bfloat16)
    block_out = stream + convolve_rows(res_halo(normed2), conv2_w, row_count)
    attn_in = apply_norm(block_out, norm_stats(block_out)).astype(jnp.bfloat16)
    mixed = block_out + attend(attn_in, qkv_w, proj_w)
    normed3 = jax.nn.silu(apply_norm(mixed, norm_stats(mixed))).astype(jnp.bfloat16)
    out_rows = with_halo(normed3, (("space", 1),), 1)
    noise_pred = jnp.transpose(convolve_rows(out_rows, conv_out_w, row_count), (3, 0, 1, 2))
    alpha_now = alphas[noise_level]
    alpha_next = alphas[noise_level - STEP]
    advanced = (
        jnp.sqrt(alpha_next / alpha_now) * (latent - jnp.sqrt(1.0 - alpha_now) * noise_pred)
        + jnp.sqrt(1.0 - alpha_next) * noise_pred
    )
    shifted = from_behind(advanced, "queue", 1)
    next_queue = jnp.where(position == 0, fresh_noise, shifted)
    return (noise_pred[None], next_queue[None])


def solution(mesh):
    in_specs = (
        P("queue", None, None, "space", None),
        P(None, None, "space", None),
        P(),
        P(),
        P(),
        P(),
        P(),
        P(),
        P(),
        P(),
        P(),
        P(),
        P(),
    )
    out_specs = (P("queue", None, None, "space", None), P("queue", None, None, "space", None))
    return jax.shard_map(
        per_device, mesh=mesh, in_specs=in_specs, out_specs=out_specs, check_vma=False
    )
```

profile of v0, /device:TPU:24, one launch (start us, length us, event | category | flops | bytes accessed | tf_op | source)
XLA Modules:
  0.0 391.2 jit_solution(11819544071218891775)
XLA Ops:
  1.8 3.8 collective-permute-start
  5.6 6.0 %collective-permute-start.1 = (bf16[4,16,1,16]{3,2,1,0:T(2,128)(2,1)S(1)}, bf16[4,16,1,16]{3,2,1,0:T(2,128)(2,1)S(1)}, u32[]{:S(2)}, u32[]{:S(2)}) collective-permute-start(bf16[4,16,1,16]{3,2,1,0:T(2,128)(2,1)S(1)} %get-tuple-element.49), channel_id=1, source_target_pairs={{1,0},{2,1},{3,2},{4,3},{5,4},{6,5},{7,6},{8,7},{9,8},{10,9},{11,1... | collective-permute-start | bytes 6152 | tf_op jit(solution)/shard_map/ppermute | solution.py:26
  32.7 32.6 %psum.56 = f32[32]{0:T(128)S(1)} all-reduce(f32[32]{0:T(128)S(1)} %reduce_sum.105), channel_id=1, replica_groups=mesh['queue'=16,'space'=16] {'space'}, use_global_device_ids=true, to_apply=%region_2.3 | all-reduce | flops 32 | bytes 256 | tf_op jit(solution)/shard_map/psum | solution.py:54
  66.4 30.7 %psum.57 = f32[32]{0:T(128)S(1)} all-reduce(f32[32]{0:T(128)S(1)} %reduce_sum.111), channel_id=1, replica_groups=mesh['queue'=16,'space'=16] {'space'}, use_global_device_ids=true, to_apply=%region_5.6 | all-reduce | flops 32 | bytes 256 | tf_op jit(solution)/shard_map/psum | solution.py:56
  97.7 4.0 %collective-permute-start.2 = (bf16[16,1,16,320]{3,2,1,0:T(8,128)(2,1)S(1)}, bf16[16,1,16,320]{3,2,1,0:T(8,128)(2,1)S(1)}, u32[]{:S(2)}, u32[]{:S(2)}) collective-permute-start(bf16[16,1,16,320]{3,2,1,0:T(8,128)(2,1)S(1)} %get-tuple-element.37), channel_id=1, source_target_pairs={{0,1},{1,2},{2,3},{3,4},{4,5},{5,6},{6,7},{7,8},{8,9},{9,10},{10,1... | collective-permute-start | bytes 491528 | tf_op jit(solution)/shard_map/ppermute | solution.py:24
  101.7 4.3 %collective-permute-start.3 = (bf16[16,1,16,320]{3,2,1,0:T(8,128)(2,1)S(1)}, bf16[16,1,16,320]{3,2,1,0:T(8,128)(2,1)S(1)}, u32[]{:S(2)}, u32[]{:S(2)}) collective-permute-start(bf16[16,1,16,320]{3,2,1,0:T(8,128)(2,1)S(1)} %get-tuple-element.38), channel_id=1, source_target_pairs={{1,0},{2,1},{3,2},{4,3},{5,4},{6,5},{7,6},{8,7},{9,8},{10,9},{11,1... | collective-permute-start | bytes 491528 | tf_op jit(solution)/shard_map/ppermute | solution.py:26
  115.4 34.9 %psum.58 = f32[32]{0:T(128)S(1)} all-reduce(f32[32]{0:T(128)S(1)} %reduce_sum.114), channel_id=1, replica_groups=mesh['queue'=16,'space'=16] {'space'}, use_global_device_ids=true, to_apply=%region_8.9 | all-reduce | flops 32 | bytes 256 | tf_op jit(solution)/shard_map/psum | solution.py:54
  152.4 30.6 %psum.59 = f32[32]{0:T(128)S(1)} all-reduce(f32[32]{0:T(128)S(1)} %reduce_sum.120), channel_id=1, replica_groups=mesh['queue'=16,'space'=16] {'space'}, use_global_device_ids=true, to_apply=%region_11.12 | all-reduce | flops 32 | bytes 256 | tf_op jit(solution)/shard_map/psum | solution.py:56
  185.0 3.9 %collective-permute-start.4 = (bf16[16,1,16,320]{3,2,1,0:T(8,128)(2,1)S(1)}, bf16[16,1,16,320]{3,2,1,0:T(8,128)(2,1)S(1)}, u32[]{:S(2)}, u32[]{:S(2)}) collective-permute-start(bf16[16,1,16,320]{3,2,1,0:T(8,128)(2,1)S(1)} %get-tuple-element.33), channel_id=1, source_target_pairs={{0,1},{1,2},{2,3},{3,4},{4,5},{5,6},{6,7},{7,8},{8,9},{9,10},{10,1... | collective-permute-start | bytes 491528 | tf_op jit(solution)/shard_map/ppermute | solution.py:24
  189.0 4.3 %collective-permute-start.5 = (bf16[16,1,16,320]{3,2,1,0:T(8,128)(2,1)S(1)}, bf16[16,1,16,320]{3,2,1,0:T(8,128)(2,1)S(1)}, u32[]{:S(2)}, u32[]{:S(2)}) collective-permute-start(bf16[16,1,16,320]{3,2,1,0:T(8,128)(2,1)S(1)} %get-tuple-element.34), channel_id=1, source_target_pairs={{1,0},{2,1},{3,2},{4,3},{5,4},{6,5},{7,6},{8,7},{9,8},{10,9},{11,1... | collective-permute-start | bytes 491528 | tf_op jit(solution)/shard_map/ppermute | solution.py:26
  201.5 2.2 fusion.137
  204.0 34.9 %psum.60 = f32[32]{0:T(128)S(1)} all-reduce(f32[32]{0:T(128)S(1)} %reduce_sum.126), channel_id=1, replica_groups=mesh['queue'=16,'space'=16] {'space'}, use_global_device_ids=true, to_apply=%region_14.15 | all-reduce | flops 32 | bytes 256 | tf_op jit(solution)/shard_map/psum | solution.py:54
  240.7 30.9 %psum.61 = f32[32]{0:T(128)S(1)} all-reduce(f32[32]{0:T(128)S(1)} %reduce_sum.154), channel_id=1, replica_groups=mesh['queue'=16,'space'=16] {'space'}, use_global_device_ids=true, to_apply=%region_17.18 | all-reduce | flops 32 | bytes 256 | tf_op jit(solution)/shard_map/psum | solution.py:56
  271.8 2.4 convolution_convert_fusion
  275.0 4.4 %reshape.268 = bf16[16,3,16,3,5,64]{5,4,3,2,1,0:T(8,128)(2,1)} reshape(bf16[768,960]{1,0:T(8,128)(2,1)S(1)} %copy.28) | data formatting | bytes 2949120 | tf_op jit(solution)/shard_map/reshape | solution.py:107
  279.4 5.4 %fusion.138 = (bf16[16,3,16,1,5,64]{5,4,3,2,1,0:T(8,128)(2,1)S(1)}, bf16[16,3,16,1,5,64]{5,4,3,2,1,0:T(8,128)(2,1)S(1)}, bf16[16,3,16,1,5,64]{5,4,3,2,1,0:T(8,128)(2,1)}) fusion(bf16[16,3,16,3,5,64]{5,4,3,2,1,0:T(8,128)(2,1)} %reshape.268), kind=kLoop, calls=%fused_computation.213 | loop fusion | bytes 2949120 | tf_op jit(solution)/shard_map/slice | solution.py:112
  284.8 4.7 %fusion.148 = (f32[3,16,5,16]{3,2,1,0:T(8,128)S(1)}, f32[3,16,5,16,16]{3,4,2,1,0:T(8,128)}) fusion(bf16[16,3,16,1,5,64]{5,4,3,2,1,0:T(8,128)(2,1)} %get-tuple-element.8, bf16[16,3,16,1,5,64]{5,4,3,2,1,0:T(8,128)(2,1)S(1)} %get-tuple-element.7), kind=kOutput, calls=%fused_computation.223 | convolution fusion | flops 8048655 | bytes 1244160 | tf_op jit(solution)/shard_map/sub | solution.py:116
  289.4 2.5 fusion.13
  293.9 2.7 copy.27
  298.7 32.6 %psum.62 = f32[32]{0:T(128)S(1)} all-reduce(f32[32]{0:T(128)S(1)} %reduce_sum.158), channel_id=1, replica_groups=mesh['queue'=16,'space'=16] {'space'}, use_global_device_ids=true, to_apply=%region_22.23 | all-reduce | flops 32 | bytes 256 | tf_op jit(solution)/shard_map/psum | solution.py:54
  331.9 30.6 %psum.63 = f32[32]{0:T(128)S(1)} all-reduce(f32[32]{0:T(128)S(1)} %reduce_sum.161), channel_id=1, replica_groups=mesh['queue'=16,'space'=16] {'space'}, use_global_device_ids=true, to_apply=%region_25.26 | all-reduce | flops 32 | bytes 256 | tf_op jit(solution)/shard_map/psum | solution.py:56
  363.2 3.9 %collective-permute-start.6 = (bf16[16,1,16,320]{3,2,1,0:T(8,128)(2,1)S(1)}, bf16[16,1,16,320]{3,2,1,0:T(8,128)(2,1)S(1)}, u32[]{:S(2)}, u32[]{:S(2)}) collective-permute-start(bf16[16,1,16,320]{3,2,1,0:T(8,128)(2,1)S(1)} %get-tuple-element.29), channel_id=1, source_target_pairs={{0,1},{1,2},{2,3},{3,4},{4,5},{5,6},{6,7},{7,8},{8,9},{9,10},{10,1... | collective-permute-start | bytes 491528 | tf_op jit(solution)/shard_map/ppermute | solution.py:24
  367.1 4.0 %collective-permute-start.7 = (bf16[16,1,16,320]{3,2,1,0:T(8,128)(2,1)S(1)}, bf16[16,1,16,320]{3,2,1,0:T(8,128)(2,1)S(1)}, u32[]{:S(2)}, u32[]{:S(2)}) collective-permute-start(bf16[16,1,16,320]{3,2,1,0:T(8,128)(2,1)S(1)} %get-tuple-element.30), channel_id=1, source_target_pairs={{1,0},{2,1},{3,2},{4,3},{5,4},{6,5},{7,6},{8,7},{9,8},{10,9},{11,1... | collective-permute-start | bytes 491528 | tf_op jit(solution)/shard_map/ppermute | solution.py:26
  382.1 7.5 %collective-permute-done.8 = f32[4,16,3,16]{3,2,1,0:T(4,128)S(1)} collective-permute-done((f32[4,16,3,16]{3,2,1,0:T(4,128)}, f32[4,16,3,16]{3,2,1,0:T(4,128)S(1)}, u32[]{:S(2)}, u32[]{:S(2)}) %collective-permute-start.8) | collective-permute-done | bytes 12320 | tf_op jit(solution)/shard_map/ppermute | solution.py:36
  (170 shorter events, 57.5 us)
Async XLA Ops:
  0.6 17.7 %copy-start = (bf16[1280,1280]{1,0:T(8,128)(2,1)S(1)}, bf16[1280,1280]{1,0:T(8,128)(2,1)}, u32[]{:S(2)}) copy-start(bf16[1280,1280]{1,0:T(8,128)(2,1)} %param.19) | copy-start | bytes 9830404
  1.8 25.9 %collective-permute-start = (bf16[4,16,1,16]{3,2,1,0:T(2,128)(2,1)S(1)}, bf16[4,16,1,16]{3,2,1,0:T(2,128)(2,1)S(1)}, u32[]{:S(2)}, u32[]{:S(2)}) collective-permute-start(bf16[4,16,1,16]{3,2,1,0:T(2,128)(2,1)S(1)} %get-tuple-element.48), channel_id=1, source_target_pairs={{0,1},{1,2},{2,3},{3,4},{4,5},{5,6},{6,7},{7,8},{8,9},{9,10},{10,1... | collective-permute-start | bytes 6152 | tf_op jit(solution)/shard_map/ppermute | solution.py:24
  5.6 22.1 %collective-permute-start.1 = (bf16[4,16,1,16]{3,2,1,0:T(2,128)(2,1)S(1)}, bf16[4,16,1,16]{3,2,1,0:T(2,128)(2,1)S(1)}, u32[]{:S(2)}, u32[]{:S(2)}) collective-permute-start(bf16[4,16,1,16]{3,2,1,0:T(2,128)(2,1)S(1)} %get-tuple-element.49), channel_id=1, source_target_pairs={{1,0},{2,1},{3,2},{4,3},{5,4},{6,5},{7,6},{8,7},{9,8},{10,9},{11,1... | collective-permute-start | bytes 6152 | tf_op jit(solution)/shard_map/ppermute | solution.py:26
  18.9 10.4 %copy-start.9 = (bf16[3,3,4,320]{3,2,1,0:T(4,128)(2,1)S(1)}, bf16[3,3,4,320]{3,2,1,0:T(4,128)(2,1)}, u32[]{:S(2)}) copy-start(bf16[3,3,4,320]{3,2,1,0:T(4,128)(2,1)} %param.17) | copy-start | bytes 69124
  65.9 31.8 %copy-start.2 = (f32[768,320]{1,0:T(8,128)}, f32[768,320]{1,0:T(8,128)S(1)}, u32[]{:S(2)}) copy-start(f32[768,320]{1,0:T(8,128)S(1)} %copy.25) | copy-start | bytes 2949124
  97.2 8.7 %copy-start.5 = (bf16[3,3,320,320]{3,2,1,0:T(8,128)(2,1)S(1)}, bf16[3,3,320,320]{3,2,1,0:T(8,128)(2,1)}, u32[]{:S(2)}) copy-start(bf16[3,3,320,320]{3,2,1,0:T(8,128)(2,1)} %param.21) | copy-start | bytes 5529604
  97.7 9.8 %collective-permute-start.2 = (bf16[16,1,16,320]{3,2,1,0:T(8,128)(2,1)S(1)}, bf16[16,1,16,320]{3,2,1,0:T(8,128)(2,1)S(1)}, u32[]{:S(2)}, u32[]{:S(2)}) collective-permute-start(bf16[16,1,16,320]{3,2,1,0:T(8,128)(2,1)S(1)} %get-tuple-element.37), channel_id=1, source_target_pairs={{0,1},{1,2},{2,3},{3,4},{4,5},{5,6},{6,7},{7,8},{8,9},{9,10},{10,1... | collective-permute-start | bytes 491528 | tf_op jit(solution)/shard_map/ppermute | solution.py:24
  101.7 7.6 %collective-permute-start.3 = (bf16[16,1,16,320]{3,2,1,0:T(8,128)(2,1)S(1)}, bf16[16,1,16,320]{3,2,1,0:T(8,128)(2,1)S(1)}, u32[]{:S(2)}, u32[]{:S(2)}) collective-permute-start(bf16[16,1,16,320]{3,2,1,0:T(8,128)(2,1)S(1)} %get-tuple-element.38), channel_id=1, source_target_pairs={{1,0},{2,1},{3,2},{4,3},{5,4},{6,5},{7,6},{8,7},{9,8},{10,9},{11,1... | collective-permute-start | bytes 491528 | tf_op jit(solution)/shard_map/ppermute | solution.py:26
  183.2 10.0 %copy-start.6 = (bf16[3,3,320,320]{3,2,1,0:T(8,128)(2,1)S(1)}, bf16[3,3,320,320]{3,2,1,0:T(8,128)(2,1)}, u32[]{:S(2)}) copy-start(bf16[3,3,320,320]{3,2,1,0:T(8,128)(2,1)} %param.22) | copy-start | bytes 5529604
  185.0 9.7 %collective-permute-start.4 = (bf16[16,1,16,320]{3,2,1,0:T(8,128)(2,1)S(1)}, bf16[16,1,16,320]{3,2,1,0:T(8,128)(2,1)S(1)}, u32[]{:S(2)}, u32[]{:S(2)}) collective-permute-start(bf16[16,1,16,320]{3,2,1,0:T(8,128)(2,1)S(1)} %get-tuple-element.33), channel_id=1, source_target_pairs={{0,1},{1,2},{2,3},{3,4},{4,5},{5,6},{6,7},{7,8},{8,9},{9,10},{10,1... | collective-permute-start | bytes 491528 | tf_op jit(solution)/shard_map/ppermute | solution.py:24
  189.0 7.6 %collective-permute-start.5 = (bf16[16,1,16,320]{3,2,1,0:T(8,128)(2,1)S(1)}, bf16[16,1,16,320]{3,2,1,0:T(8,128)(2,1)S(1)}, u32[]{:S(2)}, u32[]{:S(2)}) collective-permute-start(bf16[16,1,16,320]{3,2,1,0:T(8,128)(2,1)S(1)} %get-tuple-element.34), channel_id=1, source_target_pairs={{1,0},{2,1},{3,2},{4,3},{5,4},{6,5},{7,6},{8,7},{9,8},{10,9},{11,1... | collective-permute-start | bytes 491528 | tf_op jit(solution)/shard_map/ppermute | solution.py:26
  293.9 2.7 copy-start.3
  293.9 2.7 copy-start.4
  293.9 2.7 copy-start.8
  331.7 39.4 %copy-start.10 = (bf16[3,3,320,4]{2,3,1,0:T(4,128)(2,1)S(1)}, bf16[3,3,320,4]{2,3,1,0:T(4,128)(2,1)}, u32[]{:S(2)}) copy-start(bf16[3,3,320,4]{2,3,1,0:T(4,128)(2,1)} %param.25) | copy-start | bytes 69124
  363.2 9.7 %collective-permute-start.6 = (bf16[16,1,16,320]{3,2,1,0:T(8,128)(2,1)S(1)}, bf16[16,1,16,320]{3,2,1,0:T(8,128)(2,1)S(1)}, u32[]{:S(2)}, u32[]{:S(2)}) collective-permute-start(bf16[16,1,16,320]{3,2,1,0:T(8,128)(2,1)S(1)} %get-tuple-element.29), channel_id=1, source_target_pairs={{0,1},{1,2},{2,3},{3,4},{4,5},{5,6},{6,7},{7,8},{8,9},{9,10},{10,1... | collective-permute-start | bytes 491528 | tf_op jit(solution)/shard_map/ppermute | solution.py:24
  367.1 7.6 %collective-permute-start.7 = (bf16[16,1,16,320]{3,2,1,0:T(8,128)(2,1)S(1)}, bf16[16,1,16,320]{3,2,1,0:T(8,128)(2,1)S(1)}, u32[]{:S(2)}, u32[]{:S(2)}) collective-permute-start(bf16[16,1,16,320]{3,2,1,0:T(8,128)(2,1)S(1)} %get-tuple-element.30), channel_id=1, source_target_pairs={{1,0},{2,1},{3,2},{4,3},{5,4},{6,5},{7,6},{8,7},{9,8},{10,9},{11,1... | collective-permute-start | bytes 491528 | tf_op jit(solution)/shard_map/ppermute | solution.py:26
  377.2 1.6 copy-start.7
  377.7 13.5 %copy-start.1 = (bf16[1280,1280]{1,0:T(8,128)(2,1)S(1)}, bf16[1280,1280]{1,0:T(8,128)(2,1)}, u32[]{:S(2)}) copy-start(bf16[1280,1280]{1,0:T(8,128)(2,1)} %param.19) | copy-start | bytes 9830404
  379.5 10.1 %collective-permute-start.8 = (f32[4,16,3,16]{3,2,1,0:T(4,128)}, f32[4,16,3,16]{3,2,1,0:T(4,128)S(1)}, u32[]{:S(2)}, u32[]{:S(2)}) collective-permute-start(f32[4,16,3,16]{3,2,1,0:T(4,128)} %fusion.81), channel_id=1, source_target_pairs={{0,16},{16,32},{32,48},{48,64},{64,80},{80,96},{96,112},{112,128},... | collective-permute-start | bytes 36872 | tf_op jit(solution)/shard_map/ppermute | solution.py:36
where the time goes:
time: 392 us; the launch traced here: 391 us
  blocking collectives  258 us (66%)
  starting transfers between devices  36.2 us (9%)
  matrix products  31.4 us (8%)
  local copies, waits for them, and re-layouts  29 us (7%)
  waiting for transfers between devices  16 us (4%)
  other arithmetic  10.9 us (3%)
  between operations  9.9 us (3%)
    psum x4, blocking collectives, norm_stats(): centre = lax.psum(jnp.sum(shaped, axis=(0, 1, 2, 4)), 'space') / cell_count  135 us
    psum x4, blocking collectives, norm_stats(): lax.psum(jnp.sum((shaped - centre[:, None]) ** 2, axis=(0, 1, 2, 4)), 'sp...  123 us
    ppermute x4, starting transfers between devices, with_halo(): lax.ppermute(head, axis, [((i + 1) % count, i) for i in range(ends)])  18.6 us
    dot_general x36, matrix products, convolve_rows(): jnp.dot(window.reshape(-1, in_ch), weight[row_tap, col_tap], preferred_el...  16.6 us
    ppermute x4, starting transfers between devices, with_halo(): lax.ppermute(tail, axis, [(i, (i + 1) % count) for i in range(ends)])  15.7 us
  transfers between devices with their start and end apart: 9, of which 7 were waited for; matrix products, arithmetic and copies ran while one was open for 2% of the time, Pallas kernels for 0%

commit v1 on v0

v1 whole, which is shorter than its diff:
```python
import functools
import math

import jax
import jax.numpy as jnp
from jax import lax
from jax.experimental import pallas as pl
from jax.experimental.pallas import tpu as pltpu
from jax.sharding import PartitionSpec as P

GROUPS = 32
HEAD_DIM = 64
STEP = 50
NORM_EPS = 1e-05
MESH = pl.DeviceIdType.MESH

CH = 320
FRAMES = 16
COLS = 16
ROWS = 3
CELLS = FRAMES * COLS
PER_GROUP = CH // GROUPS
HEADS = CH // HEAD_DIM
MAIN = 256
REST = CH - MAIN
BF = jnp.bfloat16
F32 = jnp.float32


def dot(a, b):
    return jnp.dot(a, b, preferred_element_type=F32)


def dot_nt(a, b):
    return lax.dot_general(a, b, (((1,), (1,)), ((), ())), preferred_element_type=F32)


def silu_of_half(h):
    return h + h * jnp.tanh(h)


def iota(shape, dim):
    return lax.broadcasted_iota(jnp.int32, shape, dim)


def split3(v):
    hi = v.astype(BF)
    left = v - hi.astype(F32)
    mid = left.astype(BF)
    return hi, mid, (left - mid.astype(F32)).astype(BF)


def kernel(
    nq,
    ns,
    ts_ref,
    map_ref,
    lat_hbm,
    cin_hbm,
    tw1_hbm,
    tw2_hbm,
    emb_hbm,
    c1_hbm,
    c2_hbm,
    qkv_hbm,
    proj_hbm,
    cout_hbm,
    noise_ref,
    next_ref,
    lat_v,
    cin_v,
    tw1_v,
    tw2_v,
    emb_v,
    c1_v,
    c2_v,
    qkv_v,
    proj_v,
    cout_v,
    load_sem,
    lat_f,
    lat_b,
    xt,
    cin_f,
    cin_w,
    stream,
    hidden,
    block,
    xm,
    xr,
    kr,
    nr,
    wk,
    pairs,
    bias,
    cout_f,
    wout,
    attended,
    rows_st,
    stats,
    edge_raw,
    edge_scaled,
    edge_in,
    edge_next,
    main_out,
    main_in,
    lat_send,
    lat_recv,
    stat_send,
    stat_recv,
    edge_send,
    edge_recv,
    main_send,
    main_recv,
):
    q = lax.axis_index("queue")
    s = lax.axis_index("space")
    up = lax.rem(s + ns - 1, ns)
    down = lax.rem(s + 1, ns)
    ahead = lax.rem(q + 1, nq)
    behind = lax.rem(q + nq - 1, nq)
    first = s == 0
    last = s == ns - 1

    barrier = pltpu.get_barrier_semaphore()

    def greet(j, _):
        peer = lax.rem(s + j, ns)
        pl.semaphore_signal(barrier, inc=1, device_id=(q, peer), device_id_type=MESH)
        return 0

    lax.fori_loop(1, ns, greet, 0)
    for peer in (up, s, down):
        pl.semaphore_signal(barrier, inc=1, device_id=(behind, peer), device_id_type=MESH)

    loads = [
        pltpu.make_async_copy(src, dst, load_sem.at[i])
        for i, (src, dst) in enumerate(
            (
                (lat_hbm, lat_v),
                (cin_hbm, cin_v),
                (tw1_hbm, tw1_v),
                (tw2_hbm, tw2_v),
                (emb_hbm, emb_v),
                (c1_hbm, c1_v),
                (c2_hbm, c2_v),
                (qkv_hbm, qkv_v),
                (proj_hbm, proj_v),
                (cout_hbm, cout_v),
            )
        )
    ]
    for load in loads:
        load.start()
    load_lat, load_cin, load_tw1, load_tw2, load_emb, load_c1, load_c2, load_qkv, load_proj, load_cout = loads

    load_lat.wait()
    lat_f[12:16, :] = jnp.zeros((4, CELLS), F32)
    for f in range(FRAMES):
        lat_f[0:12, f * COLS : (f + 1) * COLS] = lat_v[pl.ds(f, 12, stride=FRAMES), :]
    lat_b[1] = lat_f[...].astype(BF)

    pl.semaphore_wait(barrier, ns - 1 + 3)

    lat_down = pltpu.make_async_remote_copy(
        lat_b.at[1], lat_b.at[0], lat_send.at[0], lat_recv.at[0], device_id=(q, down), device_id_type=MESH
    )
    lat_up = pltpu.make_async_remote_copy(
        lat_b.at[1], lat_b.at[2], lat_send.at[1], lat_recv.at[1], device_id=(q, up), device_id_type=MESH
    )
    lat_down.start()
    lat_up.start()

    ci = iota((CH, CH), 0) * 6554 >> 16
    cj = iota((CH, CH), 1) * 6554 >> 16
    pairs[...] = jnp.where(ci == cj, 1.0, 0.0).astype(BF)

    load_cin.wait()
    cin_f[36:40, :] = jnp.zeros((4, CH), F32)
    for a in range(3):
        for b in range(3):
            t = a * 3 + b
            cin_f[t * 4 : t * 4 + 4, :] = cin_v[a, b].astype(F32)

    kk = iota((128, 40), 0)
    jj = iota((128, 40), 1)
    tap_b = jnp.where(kk >= 36, 1, 0) + jnp.where(kk >= 72, 1, 0)
    left = kk - 36 * tap_b
    part = left * 5462 >> 16
    left = left - 12 * part
    chan = left * 21846 >> 16
    row_of = 3 * part + left - 3 * chan

    def place_cin(y, _):
        tap_a = row_of - y
        hit = (tap_a >= 0) & (tap_a < 3) & (jj == (tap_a * 3 + tap_b) * 4 + chan)
        sel = jnp.where(hit, 1.0, 0.0).astype(BF)
        cin_w[y] = dot(sel, cin_f[...].astype(BF)).astype(BF)
        return 0

    lax.fori_loop(0, 7, place_cin, 0)

    xr[:, :, 192:256] = jnp.zeros((9, CELLS, 64), BF)

    def shared_passes(which, w):
        for b in range(3):
            for a in range(3):
                kr[which, b, a * REST : (a + 1) * REST, :] = w[a, b, MAIN:CH, 0:MAIN]
            kr[which, b, 3 * REST : 256, :] = jnp.zeros((256 - 3 * REST, MAIN), BF)
        for a in range(3):
            for b in range(3):
                nr[which, a * 256 : (a + 1) * 256, b * REST : (b + 1) * REST] = w[a, b, 0:MAIN, MAIN:CH]
                nr[which, 768 + a * REST : 768 + (a + 1) * REST, b * REST : (b + 1) * REST] = w[
                    a, b, MAIN:CH, MAIN:CH
                ]
        nr[which, :, 3 * REST : 256] = jnp.zeros((1024, 256 - 3 * REST), BF)
        nr[which, 768 + 3 * REST : 1024, :] = jnp.zeros((256 - 3 * REST, 256), BF)

    lat_down.wait_recv()
    lat_up.wait_recv()
    lane = iota((16, CELLS), 1) & (COLS - 1)
    xt[108:128, :] = jnp.zeros((20, CELLS), F32)
    for n in range(3):
        v = lat_b[n].astype(F32)
        if n == 0:
            v = jnp.where(first, 0.0, v)
        if n == 2:
            v = jnp.where(last, 0.0, v)
        shifted = (
            jnp.where(lane == 0, 0.0, pltpu.roll(v, 1, 1)),
            v,
            jnp.where(lane == COLS - 1, 0.0, pltpu.roll(v, CELLS - 1, 1)),
        )
        for b in range(3):
            xt[b * 36 + n * 12 : b * 36 + n * 12 + 12, :] = shifted[b][0:12]
    x_in = xt[...].T.astype(BF)

    def row_stats(r, x):
        m = jnp.sum(x, axis=0, keepdims=True) * (1.0 / CELLS)
        rows_st[0, pl.ds(r, 1), :] = m
        rows_st[1, pl.ds(r, 1), :] = jnp.sum((x - m) ** 2, axis=0, keepdims=True)

    def send_stats(phase):
        m = rows_st[0, 0:ROWS, :]
        mean = jnp.sum(m, axis=0, keepdims=True) * (1.0 / ROWS)
        dev = jnp.sum(rows_st[1, 0:ROWS, :] + CELLS * (m - mean) ** 2, axis=0, keepdims=True)
        stats[phase, s] = jnp.concatenate([mean, dev], axis=0)

        def send(j, _):
            peer = lax.rem(s + j, ns)
            pltpu.make_async_remote_copy(
                stats.at[phase, s],
                stats.at[phase, s],
                stat_send.at[phase],
                stat_recv.at[phase],
                device_id=(q, peer),
                device_id_type=MESH,
            ).start()
            return 0

        lax.fori_loop(1, ns, send, 0)
        near = dot(jnp.broadcast_to(mean, (16, CH)).astype(BF), pairs[...])
        return near[0:1] * (1.0 / PER_GROUP)

    def take_stats(phase, near):
        pltpu.make_async_copy(
            stats.at[phase, pl.ds(0, ns - 1)], stats.at[phase, pl.ds(0, ns - 1)], stat_recv.at[phase]
        ).wait()
        v = stats[phase]
        d = v[:, 0, :] - near
        s1 = jnp.sum(d, axis=0, keepdims=True)
        s2 = jnp.sum(v[:, 1, :] + (ROWS * CELLS) * (d * d), axis=0, keepdims=True)
        parts = split3(s1) + split3(s2)
        stacked = jnp.concatenate([p.astype(F32) for p in parts] + [jnp.zeros((10, CH), F32)], axis=0)
        g = dot(stacked.astype(BF), pairs[...])
        off = (g[0:1] + g[1:2] + g[2:3]) * (1.0 / (ns * PER_GROUP))
        spread = (g[3:4] + g[4:5] + g[5:6]) * (1.0 / (ns * PER_GROUP * ROWS * CELLS)) - off * off
        return near + off, lax.rsqrt(jnp.maximum(spread, 0.0) + NORM_EPS)

    def stats_sent(phase):
        pltpu.make_async_copy(
            stats.at[phase, pl.ds(0, ns - 1)], stats.at[phase, pl.ds(0, ns - 1)], stat_send.at[phase]
        ).wait()

    def put_normed(r, y):
        yb = y.astype(BF)
        xm[r] = yb[:, 0:MAIN]
        rest = yb[:, MAIN:CH]
        xr[r + 2, :, 0:REST] = rest
        xr[r + 1, :, REST : 2 * REST] = rest
        xr[r, :, 2 * REST : 3 * REST] = rest

    def column(width, x):
        return jnp.where((iota((CELLS, width), 0) & (COLS - 1)) == x, 0.0, 1.0)

    def conv_row(which, w, y):
        x = jnp.concatenate([xm[y], xm[y + 1], xm[y + 2], xr[y + 2]], axis=1)
        z = [
            dot(
                x,
                jnp.concatenate(
                    [w[0, b, 0:MAIN, 0:MAIN], w[1, b, 0:MAIN, 0:MAIN], w[2, b, 0:MAIN, 0:MAIN], kr[which, b]], axis=0
                ),
            )
            for b in range(3)
        ]
        main = z[1] + column(MAIN, 0) * pltpu.roll(z[0], 1, 0) + column(MAIN, COLS - 1) * pltpu.roll(z[2], CELLS - 1, 0)
        zr = dot(x, nr[which])
        rest = (
            column(REST, 0) * pltpu.roll(zr, 1, 0)[:, 0:REST]
            + zr[:, REST : 2 * REST]
            + column(REST, COLS - 1) * pltpu.roll(zr, CELLS - 1, 0)[:, 2 * REST : 3 * REST]
        )
        return main, rest

    def stream_row(y):
        v = dot(x_in, cin_w[y])
        stream[y] = v
        return v

    def own_stream(i, _):
        row_stats(i, stream_row(i + 2))
        return 0

    lax.fori_loop(0, ROWS, own_stream, 0)
    near1 = send_stats(0)

    for y in (0, 1, 5, 6):
        stream_row(y)

    level = ts_ref[map_ref[q]]
    pos = iota((16, CH), 1)
    half = CH // 2
    k = jnp.where(pos < half, pos, pos - half).astype(F32)
    phases = level.astype(F32) * jnp.exp(k * (-math.log(10000.0) / half))
    sinusoid = jnp.where(pos < half, jnp.cos(phases), jnp.sin(phases)).astype(BF)
    load_tw1.wait()
    h = dot(sinusoid, tw1_v[...])
    first_hidden = silu_of_half(0.5 * h).astype(BF)
    load_tw2.wait()
    h = dot(first_hidden, tw2_v[...])
    second = silu_of_half(0.5 * h).astype(BF)
    load_emb.wait()
    bias[...] = dot_nt(second, emb_v[...])[0:1]
    load_c1.wait()
    shared_passes(0, c1_v)

    mean, inv = take_stats(0, near1)
    half_inv = 0.5 * inv

    def norm1(r, _):
        y = silu_of_half((stream[r] - mean) * half_inv)
        row = s * ROWS + r - 2
        put_normed(r, jnp.where((row >= 0) & (row < ns * ROWS), y, 0.0))
        return 0

    lax.fori_loop(0, 7, norm1, 0)

    def hidden_row(j):
        main, rest = conv_row(0, c1_v, j)
        hidden[j, :, 0:MAIN] = main + bias[:, 0:MAIN]
        hidden[j, :, MAIN:CH] = rest + bias[:, MAIN:CH]

    def own_hidden(i, _):
        hidden_row(i + 1)
        row_stats(i, hidden[i + 1])
        return 0

    lax.fori_loop(0, ROWS, own_hidden, 0)
    near2 = send_stats(1)

    def halo_hidden(i, _):
        hidden_row(i * 4)
        return 0

    lax.fori_loop(0, 2, halo_hidden, 0)
    load_c2.wait()
    shared_passes(1, c2_v)

    mean2, inv2 = take_stats(1, near2)
    half_inv2 = 0.5 * inv2

    def norm2(r, _):
        y = silu_of_half((hidden[r] - mean2) * half_inv2)
        row = s * ROWS + r - 1
        put_normed(r, jnp.where((row >= 0) & (row < ns * ROWS), y, 0.0))
        return 0

    lax.fori_loop(0, 5, norm2, 0)

    def block_row(i, _):
        main, rest = conv_row(1, c2_v, i)
        block[i, :, 0:MAIN] = stream[i + 2, :, 0:MAIN] + main
        block[i, :, MAIN:CH] = stream[i + 2, :, MAIN:CH] + rest
        row_stats(i, block[i])
        return 0

    lax.fori_loop(0, ROWS, block_row, 0)
    near3 = send_stats(2)

    load_qkv.wait()
    wk[...] = qkv_v[:, CH : 2 * CH]
    load_proj.wait()
    load_cout.wait()
    cout_f[36:40, :] = jnp.zeros((4, CH), F32)
    for a in range(3):
        for b in range(3):
            r = (a * 3 + b) * 4
            cout_f[r : r + 4, :] = cout_v[a, b].astype(F32)
    to = iota((144, 40), 0)
    src = iota((144, 40), 1)
    to_b = jnp.where(to >= 48, 1, 0) + jnp.where(to >= 96, 1, 0)
    to_part = to - 48 * to_b >> 4
    to_row = to & 15
    to_c = to_row * 21846 >> 16
    to_y = to_row - 3 * to_c + jnp.where(to_part == 1, ROWS, 0) - jnp.where(to_part == 2, ROWS, 0)
    for i in range(ROWS):
        tap = i - to_y + 1
        hit = (tap >= 0) & (tap < 3) & (to_row < 12) & (src == (tap * 3 + to_b) * 4 + to_c)
        wout[i] = dot(jnp.where(hit, 1.0, 0.0).astype(BF), cout_f[...].astype(BF)).astype(BF)

    step_of = iota((8, 128), 0) * 128 + iota((8, 128), 1)
    lo, hi = 0.00085**0.5, 0.012**0.5
    beta = (lo + step_of.astype(F32) * ((hi - lo) / 999.0)) ** 2

    def alpha(t):
        v = jnp.where(step_of <= t, 1.0 - beta, 1.0)
        for sh in (64, 32, 16, 8, 4, 2, 1):
            v = v * pltpu.roll(v, sh, 1)
        for sh in (4, 2, 1):
            v = v * pltpu.roll(v, sh, 0)
        return v[0:1, 0:1]

    alpha_now = alpha(level)
    alpha_next = alpha(level - STEP)
    keep = jnp.sqrt(alpha_next / alpha_now)
    gain = jnp.sqrt(1.0 - alpha_next) - keep * jnp.sqrt(1.0 - alpha_now)

    mean3, inv3 = take_stats(2, near3)

    same = ((iota((CELLS, CELLS), 0) ^ iota((CELLS, CELLS), 1)) & (COLS - 1)) == 0
    low_half = iota((CELLS, 128), 1) < HEAD_DIM

    def attend_row(i, _):
        x = ((block[i] - mean3) * inv3).astype(BF)
        query = (dot(x, qkv_v[:, 0:CH]) * HEAD_DIM**-0.5).astype(BF)
        key = dot(x, wk[...]).astype(BF)
        value = dot(x, qkv_v[:, 2 * CH : 3 * CH]).astype(BF)
        ones = jnp.ones((CELLS, 128), BF)
        for t in range(3):
            width = min(128, CH - t * 128)
            lanes = slice(t * 128, t * 128 + width)
            qt, kt, vt = query[:, lanes], key[:, lanes], value[:, lanes]
            if width < 128:
                vt = jnp.concatenate([vt, jnp.zeros((CELLS, 128 - width), BF)], axis=1)
            vt = jnp.concatenate([vt, ones], axis=1)
            outs = []
            for part in range(width // HEAD_DIM):
                qh = qt
                if width == 128:
                    qh = jnp.where(low_half if part == 0 else jnp.logical_not(low_half), qt, jnp.zeros_like(qt))
                sc = jnp.where(same, dot_nt(qh, kt), -1e30)
                p = jnp.exp(sc - jnp.max(sc, axis=1, keepdims=True)).astype(BF)
                o = dot(p, vt)
                outs.append(o[:, 0:128] / o[:, 128:256])
            o = outs[0] if len(outs) == 1 else jnp.where(low_half, outs[0], outs[1])
            attended[:, lanes] = o[:, 0:width].astype(BF)
        mixed = block[i] + dot(attended[...], proj_v[...])
        block[i] = mixed
        row_stats(i, mixed)
        return 0

    lax.fori_loop(0, ROWS, attend_row, 0)
    near4 = send_stats(3)
    mean4, inv4 = take_stats(3, near4)
    half_inv4 = 0.5 * inv4

    z = jnp.zeros((144, CELLS), F32)
    for i in range(ROWS):
        z = z + dot_nt(wout[i], silu_of_half((block[i] - mean4) * half_inv4).astype(BF))
    lane = iota((48, CELLS), 1) & (COLS - 1)
    sums = (
        z[48:96]
        + jnp.where(lane == 0, 0.0, pltpu.roll(z[0:48], 1, 1))
        + jnp.where(lane == COLS - 1, 0.0, pltpu.roll(z[96:144], CELLS - 1, 1))
    )
    own = sums[0:16]
    for side in range(2):
        edge_raw[side] = sums[16 + 16 * side : 32 + 16 * side]
        edge_scaled[side] = gain * sums[16 + 16 * side : 32 + 16 * side]
    sends = []
    for side, peer in ((0, down), (1, up)):
        sends.append(
            pltpu.make_async_remote_copy(
                edge_scaled.at[side],
                edge_next.at[side],
                edge_send.at[side],
                edge_recv.at[side],
                device_id=(ahead, peer),
                device_id_type=MESH,
            )
        )
        sends.append(
            pltpu.make_async_remote_copy(
                edge_raw.at[side],
                edge_in.at[side],
                edge_send.at[2 + side],
                edge_recv.at[2 + side],
                device_id=(q, peer),
                device_id_type=MESH,
            )
        )
    for send in sends:
        send.start()
    main_out[...] = keep * lat_f[...] + gain * own
    main_send_copy = pltpu.make_async_remote_copy(
        main_out, main_in, main_send, main_recv, device_id=(ahead, s), device_id_type=MESH
    )
    main_send_copy.start()

    def put(out, v):
        for f in range(FRAMES):
            out[pl.ds(f, 12, stride=FRAMES), :] = v[0:12, f * COLS : (f + 1) * COLS]

    sends[1].wait_recv()
    sends[3].wait_recv()
    put(noise_ref, own + jnp.where(first, 0.0, edge_in[0]) + jnp.where(last, 0.0, edge_in[1]))
    main_send_copy.wait_recv()
    sends[0].wait_recv()
    sends[2].wait_recv()
    put(next_ref, main_in[...] + jnp.where(first, 0.0, edge_next[0]) + jnp.where(last, 0.0, edge_next[1]))

    lat_down.wait_send()
    lat_up.wait_send()
    for phase in range(4):
        stats_sent(phase)
    for send in sends:
        send.wait_send()
    main_send_copy.wait_send()


def per_device(
    nq,
    ns,
    latents,
    fresh_noise,
    timesteps,
    queue_map,
    conv_in_w,
    time_w1,
    time_w2,
    emb_w,
    conv1_w,
    conv2_w,
    qkv_w,
    proj_w,
    conv_out_w,
):
    smem = pl.BlockSpec(memory_space=pltpu.SMEM)
    hbm = pl.BlockSpec(memory_space=pl.ANY)
    vmem = pl.BlockSpec(memory_space=pltpu.VMEM)
    latents = jnp.transpose(latents[0], (0, 2, 1, 3)).reshape(4 * ROWS * FRAMES, COLS)
    emb_t = emb_w.T
    out_t = jnp.swapaxes(conv_out_w, 2, 3)
    weights = (conv_in_w, time_w1, time_w2, emb_t, conv1_w, conv2_w, qkv_w, proj_w, out_t)
    DMA = pltpu.SemaphoreType.DMA
    noise, nxt = pl.pallas_call(
        functools.partial(kernel, nq, ns),
        out_shape=(
            jax.ShapeDtypeStruct((4 * ROWS * FRAMES, COLS), F32),
            jax.ShapeDtypeStruct((4 * ROWS * FRAMES, COLS), F32),
        ),
        in_specs=[smem, smem] + [hbm] * (1 + len(weights)),
        out_specs=(vmem, vmem),
        scratch_shapes=[pltpu.VMEM(latents.shape, F32)]
        + [pltpu.VMEM(w.shape, BF) for w in weights]
        + [
            DMA((1 + len(weights),)),
            pltpu.VMEM((16, CELLS), F32),
            pltpu.VMEM((3, 16, CELLS), BF),
            pltpu.VMEM((128, CELLS), F32),
            pltpu.VMEM((40, CH), F32),
            pltpu.VMEM((7, 128, CH), BF),
            pltpu.VMEM((7, CELLS, CH), F32),
            pltpu.VMEM((5, CELLS, CH), F32),
            pltpu.VMEM((3, CELLS, CH), F32),
            pltpu.VMEM((7, CELLS, MAIN), BF),
            pltpu.VMEM((9, CELLS, 256), BF),
            pltpu.VMEM((2, 3, 256, MAIN), BF),
            pltpu.VMEM((2, 1024, 256), BF),
            pltpu.VMEM((CH, CH), BF),
            pltpu.VMEM((CH, CH), BF),
            pltpu.VMEM((1, CH), F32),
            pltpu.VMEM((40, CH), F32),
            pltpu.VMEM((3, 144, CH), BF),
            pltpu.VMEM((CELLS, CH), BF),
            pltpu.VMEM((2, 8, CH), F32),
            pltpu.VMEM((4, ns, 2, CH), F32),
            pltpu.VMEM((2, 16, CELLS), F32),
            pltpu.VMEM((2, 16, CELLS), F32),
            pltpu.VMEM((2, 16, CELLS), F32),
            pltpu.VMEM((2, 16, CELLS), F32),
            pltpu.VMEM((16, CELLS), F32),
            pltpu.VMEM((16, CELLS), F32),
            DMA((2,)),
            DMA((2,)),
            DMA((4,)),
            DMA((4,)),
            DMA((4,)),
            DMA((4,)),
            DMA,
            DMA,
        ],
        compiler_params=pltpu.CompilerParams(
            collective_id=0, has_side_effects=True, vmem_limit_bytes=60 * 1024 * 1024
        ),
        cost_estimate=pl.CostEstimate(flops=10**10, bytes_accessed=10**7, transcendentals=10**6),
    )(timesteps, queue_map, latents, *weights)

    def as_frames(v):
        return jnp.transpose(v.reshape(4, ROWS, FRAMES, COLS), (0, 2, 1, 3))

    next_queue = jnp.where(lax.axis_index("queue") == 0, fresh_noise, as_frames(nxt))
    return as_frames(noise)[None], next_queue[None]


def solution(mesh):
    nq, ns = mesh.shape["queue"], mesh.shape["space"]
    rows = P("queue", None, None, "space", None)
    return jax.shard_map(
        functools.partial(per_device, nq, ns),
        mesh=mesh,
        in_specs=(rows, P(None, None, "space", None)) + (P(),) * 11,
        out_specs=(rows, rows),
        check_vma=False,
    )
```

time: 392 us -> 55.9 us (0.14)
  the two profiles are of different devices: /device:TPU:24 before, /device:TPU:1 now
where the time goes in v1:
time: 55.9 us; the launch traced here: 55.7 us
  Pallas kernels  52 us (93%)
  other arithmetic  1.56 us (3%)
  local copies, waits for them, and re-layouts  1.54 us (3%)
  between operations  0.67 us (1%)
    pallas_call x1, Pallas kernels, per_device(): pl.pallas_call(functools.partial(kernel, nq, ns), out_shape=(jax.ShapeDty...  52 us
    broadcast_in_dim x1, other arithmetic, per_device(): return (as_frames(noise)[None], next_queue[None])  1.56 us
    unnamed x3, local copies, waits for them, and re-layouts  1.54 us

profile of v1, /device:TPU:1, one launch (start us, length us, event | category | flops | bytes accessed | tf_op | source)
XLA Modules:
  0.0 55.7 jit_solution(5571109398441210148)
XLA Ops:
  0.6 0.0 copy-start
  0.7 52.0 %shard_map.140 = (f32[192,16]{1,0:T(8,128)}, f32[192,16]{1,0:T(8,128)}) custom-call(s32[16]{0:T(128)} %ts_ref.1, s32[16]{0:T(128)} %map_ref.1, f32[192,16]{1,0:T(8,128)} %bitcast.20, bf16[3,3,4,320]{3,2,1,0:T(4,128)(2,1)} %cin_hbm.1, bf16[320,1280]{1,0:T(8,128)(2,1)} %tw1_hbm.1, bf16[1280,1280]{1,0:T(8,128)(2,1)} %tw2_hbm.1, bf16[320,1280]{1,0:T(8,128)(2,1)} %bitcast.19, ...), custom_call_target="tpu_custom_call" | custom-call | flops 10000000000 | bytes 10000000 | tf_op jit(solution)/shard_map/pallas_call | solution.py:567
  52.6 0.0 copy-done
  52.6 1.6 %select_bitcast_fusion = f32[1,4,16,3,16]{4,2,3,1,0:T(8,128)} fusion(f32[4,16,3,16]{3,1,2,0:T(8,128)S(1)} %copy-done, f32[4,16,3,16]{3,1,2,0:T(8,128)} %bitcast.18, pred[]{:T(512)S(6)} %eq.3), kind=kLoop, calls=%fused_computation | loop fusion | flops 3072 | bytes 36865 | tf_op jit(solution)/shard_map/broadcast_in_dim | solution.py:624
  54.2 1.5 %copy.16 = f32[1,4,16,3,16]{4,2,3,1,0:T(8,128)} copy(f32[1,4,16,3,16]{4,2,3,1,0:T(8,128)} %bitcast.17) | data formatting | bytes 24576
Async XLA Ops:
  0.6 52.0 %copy-start = (f32[4,16,3,16]{3,1,2,0:T(8,128)S(1)}, f32[4,16,3,16]{3,1,2,0:T(8,128)}, u32[]{:S(2)}) copy-start(f32[4,16,3,16]{3,1,2,0:T(8,128)} %param.14) | copy-start | bytes 36868

commit v2 on v1

--- a/solution.py
+++ b/solution.py
@@ -53,8 +53,8 @@
 def kernel(
     nq,
     ns,
-    ts_ref,
-    map_ref,
+    ts_hbm,
+    map_hbm,
     lat_hbm,
     cin_hbm,
     tw1_hbm,
@@ -67,6 +67,8 @@
     cout_hbm,
     noise_ref,
     next_ref,
+    ts_ref,
+    map_ref,
     lat_v,
     cin_v,
     tw1_v,
@@ -90,7 +92,9 @@
     xr,
     kr,
     nr,
-    wk,
+    wqkv,
+    wproj,
+    projected,
     pairs,
     bias,
     cout_f,
@@ -119,6 +123,8 @@
     down = lax.rem(s + 1, ns)
     ahead = lax.rem(q + 1, nq)
     behind = lax.rem(q + nq - 1, nq)
+    ring = ns // 2
+    order = sorted(range(1, ns), key=lambda j: -min(j % ring, ring - j % ring))
     first = s == 0
     last = s == ns - 1
 
@@ -147,12 +153,14 @@
                 (qkv_hbm, qkv_v),
                 (proj_hbm, proj_v),
                 (cout_hbm, cout_v),
+                (ts_hbm, ts_ref),
+                (map_hbm, map_ref),
             )
         )
     ]
     for load in loads:
         load.start()
-    load_lat, load_cin, load_tw1, load_tw2, load_emb, load_c1, load_c2, load_qkv, load_proj, load_cout = loads
+    load_lat, load_cin, load_tw1, load_tw2, load_emb, load_c1, load_c2, load_qkv, load_proj, load_cout, load_ts, load_map = loads
 
     load_lat.wait()
     lat_f[12:16, :] = jnp.zeros((4, CELLS), F32)
@@ -200,7 +208,7 @@
 
     lax.fori_loop(0, 7, place_cin, 0)
 
-    xr[:, :, 192:256] = jnp.zeros((9, CELLS, 64), BF)
+    xr[:, 192:256] = jnp.zeros((9 * CELLS, 64), BF)
 
     def shared_passes(which, w):
         for b in range(3):
@@ -235,6 +243,9 @@
             xt[b * 36 + n * 12 : b * 36 + n * 12 + 12, :] = shifted[b][0:12]
     x_in = xt[...].T.astype(BF)
 
+    def cells(r, n=1):
+        return pl.ds(r * CELLS if isinstance(r, int) else pl.multiple_of(r * CELLS, CELLS), n * CELLS)
+
     def row_stats(r, x):
         m = jnp.sum(x, axis=0, keepdims=True) * (1.0 / CELLS)
         rows_st[0, pl.ds(r, 1), :] = m
@@ -246,19 +257,15 @@
         dev = jnp.sum(rows_st[1, 0:ROWS, :] + CELLS * (m - mean) ** 2, axis=0, keepdims=True)
         stats[phase, s] = jnp.concatenate([mean, dev], axis=0)
 
-        def send(j, _):
-            peer = lax.rem(s + j, ns)
+        for j in order:
             pltpu.make_async_remote_copy(
                 stats.at[phase, s],
                 stats.at[phase, s],
                 stat_send.at[phase],
                 stat_recv.at[phase],
-                device_id=(q, peer),
+                device_id=(q, lax.rem(s + j, ns)),
                 device_id_type=MESH,
             ).start()
-            return 0
-
-        lax.fori_loop(1, ns, send, 0)
         near = dot(jnp.broadcast_to(mean, (16, CH)).astype(BF), pairs[...])
         return near[0:1] * (1.0 / PER_GROUP)
 
@@ -267,9 +274,11 @@
             stats.at[phase, pl.ds(0, ns - 1)], stats.at[phase, pl.ds(0, ns - 1)], stat_recv.at[phase]
         ).wait()
         v = stats[phase]
-        d = v[:, 0, :] - near
-        s1 = jnp.sum(d, axis=0, keepdims=True)
-        s2 = jnp.sum(v[:, 1, :] + (ROWS * CELLS) * (d * d), axis=0, keepdims=True)
+        d = v - jnp.concatenate([near, jnp.zeros_like(near)], axis=0)
+        total = jnp.sum(d, axis=0)
+        square = jnp.sum(d * d, axis=0)
+        s1 = total[0:1]
+        s2 = total[1:2] + (ROWS * CELLS) * square[0:1]
         parts = split3(s1) + split3(s2)
         stacked = jnp.concatenate([p.astype(F32) for p in parts] + [jnp.zeros((10, CH), F32)], axis=0)
         g = dot(stacked.astype(BF), pairs[...])
@@ -284,17 +293,23 @@
 
     def put_normed(r, y):
         yb = y.astype(BF)
-        xm[r] = yb[:, 0:MAIN]
+        xm[cells(r), :] = yb[:, 0:MAIN]
         rest = yb[:, MAIN:CH]
-        xr[r + 2, :, 0:REST] = rest
-        xr[r + 1, :, REST : 2 * REST] = rest
-        xr[r, :, 2 * REST : 3 * REST] = rest
-
-    def column(width, x):
-        return jnp.where((iota((CELLS, width), 0) & (COLS - 1)) == x, 0.0, 1.0)
-
-    def conv_row(which, w, y):
-        x = jnp.concatenate([xm[y], xm[y + 1], xm[y + 2], xr[y + 2]], axis=1)
+        xr[cells(r + 2), 0:REST] = rest
+        xr[cells(r + 1), REST : 2 * REST] = rest
+        xr[cells(r), 2 * REST : 3 * REST] = rest
+
+    def column(n, width, x):
+        return jnp.where((iota((n * CELLS, width), 0) & (COLS - 1)) == x, 0.0, 1.0)
+
+    def conv_rows(which, w, rows):
+        n = len(rows)
+        size = n * CELLS
+
+        def window(ref, a):
+            return jnp.concatenate([ref[cells(y + a), :] for y in rows], axis=0)
+
+        x = jnp.concatenate([window(xm, 0), window(xm, 1), window(xm, 2), window(xr, 2)], axis=1)
         z = [
             dot(
                 x,
@@ -304,18 +319,20 @@
             )
             for b in range(3)
         ]
-        main = z[1] + column(MAIN, 0) * pltpu.roll(z[0], 1, 0) + column(MAIN, COLS - 1) * pltpu.roll(z[2], CELLS - 1, 0)
+        main = (
+            z[1] + column(n, MAIN, 0) * pltpu.roll(z[0], 1, 0) + column(n, MAIN, COLS - 1) * pltpu.roll(z[2], size - 1, 0)
+        )
         zr = dot(x, nr[which])
         rest = (
-            column(REST, 0) * pltpu.roll(zr, 1, 0)[:, 0:REST]
+            column(n, REST, 0) * pltpu.roll(zr, 1, 0)[:, 0:REST]
             + zr[:, REST : 2 * REST]
-            + column(REST, COLS - 1) * pltpu.roll(zr, CELLS - 1, 0)[:, 2 * REST : 3 * REST]
+            + column(n, REST, COLS - 1) * pltpu.roll(zr, size - 1, 0)[:, 2 * REST : 3 * REST]
         )
         return main, rest
 
     def stream_row(y):
         v = dot(x_in, cin_w[y])
-        stream[y] = v
+        stream[cells(y), :] = v
         return v
 
     def own_stream(i, _):
@@ -328,6 +345,8 @@
     for y in (0, 1, 5, 6):
         stream_row(y)
 
+    load_ts.wait()
+    load_map.wait()
     level = ts_ref[map_ref[q]]
     pos = iota((16, CH), 1)
     half = CH // 2
@@ -349,31 +368,27 @@
     half_inv = 0.5 * inv
 
     def norm1(r, _):
-        y = silu_of_half((stream[r] - mean) * half_inv)
+        y = silu_of_half((stream[cells(r), :] - mean) * half_inv)
         row = s * ROWS + r - 2
         put_normed(r, jnp.where((row >= 0) & (row < ns * ROWS), y, 0.0))
         return 0
 
-    lax.fori_loop(0, 7, norm1, 0)
-
-    def hidden_row(j):
-        main, rest = conv_row(0, c1_v, j)
-        hidden[j, :, 0:MAIN] = main + bias[:, 0:MAIN]
-        hidden[j, :, MAIN:CH] = rest + bias[:, MAIN:CH]
-
-    def own_hidden(i, _):
-        hidden_row(i + 1)
-        row_stats(i, hidden[i + 1])
-        return 0
-
-    lax.fori_loop(0, ROWS, own_hidden, 0)
+    lax.fori_loop(1, 6, norm1, 0)
+
+    def hidden_rows(rows):
+        main, rest = conv_rows(0, c1_v, rows)
+        for i, j in enumerate(rows):
+            hidden[cells(j), 0:MAIN] = main[i * CELLS : (i + 1) * CELLS] + bias[:, 0:MAIN]
+            hidden[cells(j), MAIN:CH] = rest[i * CELLS : (i + 1) * CELLS] + bias[:, MAIN:CH]
+
+    hidden_rows((1, 2, 3))
+    for i in range(ROWS):
+        row_stats(i, hidden[cells(i + 1), :])
     near2 = send_stats(1)
 
-    def halo_hidden(i, _):
-        hidden_row(i * 4)
-        return 0
-
-    lax.fori_loop(0, 2, halo_hidden, 0)
+    norm1(0, 0)
+    norm1(6, 0)
+    hidden_rows((0, 4))
     load_c2.wait()
     shared_passes(1, c2_v)
 
@@ -381,26 +396,27 @@
     half_inv2 = 0.5 * inv2
 
     def norm2(r, _):
-        y = silu_of_half((hidden[r] - mean2) * half_inv2)
+        y = silu_of_half((hidden[cells(r), :] - mean2) * half_inv2)
         row = s * ROWS + r - 1
         put_normed(r, jnp.where((row >= 0) & (row < ns * ROWS), y, 0.0))
         return 0
 
     lax.fori_loop(0, 5, norm2, 0)
 
-    def block_row(i, _):
-        main, rest = conv_row(1, c2_v, i)
-        block[i, :, 0:MAIN] = stream[i + 2, :, 0:MAIN] + main
-        block[i, :, MAIN:CH] = stream[i + 2, :, MAIN:CH] + rest
-        row_stats(i, block[i])
-        return 0
-
-    lax.fori_loop(0, ROWS, block_row, 0)
+    main, rest = conv_rows(1, c2_v, (0, 1, 2))
+    block[:, 0:MAIN] = stream[cells(2, ROWS), 0:MAIN] + main
+    block[:, MAIN:CH] = stream[cells(2, ROWS), MAIN:CH] + rest
+    for i in range(ROWS):
+        row_stats(i, block[cells(i), :])
     near3 = send_stats(2)
 
     load_qkv.wait()
-    wk[...] = qkv_v[:, CH : 2 * CH]
+    wqkv[:, 0:CH] = qkv_v[:, 0:CH] * jnp.asarray(HEAD_DIM**-0.5, BF)
+    wqkv[:, CH:384] = jnp.zeros((CH, 384 - CH), BF)
+    wqkv[:, 384:1024] = qkv_v[:, CH : 3 * CH]
     load_proj.wait()
+    wproj[0:64, :] = jnp.zeros((64, CH), BF)
+    wproj[64:384, :] = proj_v[...]
     load_cout.wait()
     cout_f[36:40, :] = jnp.zeros((4, CH), F32)
     for a in range(3):
@@ -441,43 +457,39 @@
     same = ((iota((CELLS, CELLS), 0) ^ iota((CELLS, CELLS), 1)) & (COLS - 1)) == 0
     low_half = iota((CELLS, 128), 1) < HEAD_DIM
 
+    projected[...] = dot(((block[...] - mean3) * inv3).astype(BF), wqkv[...]).astype(BF)
+
     def attend_row(i, _):
-        x = ((block[i] - mean3) * inv3).astype(BF)
-        query = (dot(x, qkv_v[:, 0:CH]) * HEAD_DIM**-0.5).astype(BF)
-        key = dot(x, wk[...]).astype(BF)
-        value = dot(x, qkv_v[:, 2 * CH : 3 * CH]).astype(BF)
+        row = cells(i)
         ones = jnp.ones((CELLS, 128), BF)
-        for t in range(3):
-            width = min(128, CH - t * 128)
-            lanes = slice(t * 128, t * 128 + width)
-            qt, kt, vt = query[:, lanes], key[:, lanes], value[:, lanes]
-            if width < 128:
-                vt = jnp.concatenate([vt, jnp.zeros((CELLS, 128 - width), BF)], axis=1)
-            vt = jnp.concatenate([vt, ones], axis=1)
-            outs = []
-            for part in range(width // HEAD_DIM):
-                qh = qt
-                if width == 128:
-                    qh = jnp.where(low_half if part == 0 else jnp.logical_not(low_half), qt, jnp.zeros_like(qt))
-                sc = jnp.where(same, dot_nt(qh, kt), -1e30)
-                p = jnp.exp(sc - jnp.max(sc, axis=1, keepdims=True)).astype(BF)
-                o = dot(p, vt)
-                outs.append(o[:, 0:128] / o[:, 128:256])
-            o = outs[0] if len(outs) == 1 else jnp.where(low_half, outs[0], outs[1])
-            attended[:, lanes] = o[:, 0:width].astype(BF)
-        mixed = block[i] + dot(attended[...], proj_v[...])
-        block[i] = mixed
-        row_stats(i, mixed)
+
+        def head(h):
+            qt = projected[row, h // 2 * 128 : h // 2 * 128 + 128]
+            if h < HEADS - 1:
+                qt = jnp.where(low_half if h % 2 == 0 else jnp.logical_not(low_half), qt, jnp.zeros_like(qt))
+            kt = projected[row, 384 + h // 2 * 128 : 512 + h // 2 * 128]
+            vt = projected[row, 640 + (h + 1) // 2 * 128 : 768 + (h + 1) // 2 * 128]
+            sc = jnp.where(same, dot_nt(qt, kt), -1e30)
+            p = jnp.exp(sc - jnp.max(sc, axis=1, keepdims=True)).astype(BF)
+            o = dot(p, jnp.concatenate([vt, ones], axis=1))
+            return o[:, 0:128] / o[:, 128:256]
+
+        attended[row, 0:128] = jnp.where(low_half, 0.0, head(0)).astype(BF)
+        attended[row, 128:256] = jnp.where(low_half, head(1), head(2)).astype(BF)
+        attended[row, 256:384] = jnp.where(low_half, head(3), head(4)).astype(BF)
         return 0
 
     lax.fori_loop(0, ROWS, attend_row, 0)
+    block[...] += dot(attended[...], wproj[...])
+    for i in range(ROWS):
+        row_stats(i, block[cells(i), :])
     near4 = send_stats(3)
     mean4, inv4 = take_stats(3, near4)
     half_inv4 = 0.5 * inv4
 
     z = jnp.zeros((144, CELLS), F32)
     for i in range(ROWS):
-        z = z + dot_nt(wout[i], silu_of_half((block[i] - mean4) * half_inv4).astype(BF))
+        z = z + dot_nt(wout[i], silu_of_half((block[cells(i), :] - mean4) * half_inv4).astype(BF))
     lane = iota((48, CELLS), 1) & (COLS - 1)
     sums = (
         z[48:96]
@@ -556,44 +568,49 @@
     proj_w,
     conv_out_w,
 ):
-    smem = pl.BlockSpec(memory_space=pltpu.SMEM)
-    hbm = pl.BlockSpec(memory_space=pl.ANY)
+    hbm = pl.BlockSpec(memory_space=pltpu.HBM)
     vmem = pl.BlockSpec(memory_space=pltpu.VMEM)
     latents = jnp.transpose(latents[0], (0, 2, 1, 3)).reshape(4 * ROWS * FRAMES, COLS)
     emb_t = emb_w.T
     out_t = jnp.swapaxes(conv_out_w, 2, 3)
     weights = (conv_in_w, time_w1, time_w2, emb_t, conv1_w, conv2_w, qkv_w, proj_w, out_t)
     DMA = pltpu.SemaphoreType.DMA
+    operands = [
+        pltpu.with_memory_space_constraint(v, pltpu.HBM) for v in (timesteps, queue_map, latents, *weights)
+    ]
     noise, nxt = pl.pallas_call(
         functools.partial(kernel, nq, ns),
         out_shape=(
             jax.ShapeDtypeStruct((4 * ROWS * FRAMES, COLS), F32),
             jax.ShapeDtypeStruct((4 * ROWS * FRAMES, COLS), F32),
         ),
-        in_specs=[smem, smem] + [hbm] * (1 + len(weights)),
+        in_specs=[hbm] * len(operands),
         out_specs=(vmem, vmem),
-        scratch_shapes=[pltpu.VMEM(latents.shape, F32)]
+        scratch_shapes=[pltpu.SMEM(timesteps.shape, jnp.int32), pltpu.SMEM(queue_map.shape, jnp.int32)]
+        + [pltpu.VMEM(latents.shape, F32)]
         + [pltpu.VMEM(w.shape, BF) for w in weights]
         + [
-            DMA((1 + len(weights),)),
+            DMA((len(operands),)),
             pltpu.VMEM((16, CELLS), F32),
             pltpu.VMEM((3, 16, CELLS), BF),
             pltpu.VMEM((128, CELLS), F32),
             pltpu.VMEM((40, CH), F32),
             pltpu.VMEM((7, 128, CH), BF),
-            pltpu.VMEM((7, CELLS, CH), F32),
-            pltpu.VMEM((5, CELLS, CH), F32),
-            pltpu.VMEM((3, CELLS, CH), F32),
-            pltpu.VMEM((7, CELLS, MAIN), BF),
-            pltpu.VMEM((9, CELLS, 256), BF),
+            pltpu.VMEM((7 * CELLS, CH), F32),
+            pltpu.VMEM((5 * CELLS, CH), F32),
+            pltpu.VMEM((3 * CELLS, CH), F32),
+            pltpu.VMEM((7 * CELLS, MAIN), BF),
+            pltpu.VMEM((9 * CELLS, 256), BF),
             pltpu.VMEM((2, 3, 256, MAIN), BF),
             pltpu.VMEM((2, 1024, 256), BF),
-            pltpu.VMEM((CH, CH), BF),
+            pltpu.VMEM((CH, 1024), BF),
+            pltpu.VMEM((384, CH), BF),
+            pltpu.VMEM((ROWS * CELLS, 1024), BF),
             pltpu.VMEM((CH, CH), BF),
             pltpu.VMEM((1, CH), F32),
             pltpu.VMEM((40, CH), F32),
             pltpu.VMEM((3, 144, CH), BF),
-            pltpu.VMEM((CELLS, CH), BF),
+            pltpu.VMEM((ROWS * CELLS, 384), BF),
             pltpu.VMEM((2, 8, CH), F32),
             pltpu.VMEM((4, ns, 2, CH), F32),
             pltpu.VMEM((2, 16, CELLS), F32),
@@ -612,10 +629,10 @@
             DMA,
         ],
         compiler_params=pltpu.CompilerParams(
-            collective_id=0, has_side_effects=True, vmem_limit_bytes=60 * 1024 * 1024
+            collective_id=0, has_side_effects=True, vmem_limit_bytes=44 * 1024 * 1024
         ),
         cost_estimate=pl.CostEstimate(flops=10**10, bytes_accessed=10**7, transcendentals=10**6),
-    )(timesteps, queue_map, latents, *weights)
+    )(*operands)
 
     def as_frames(v):
         return jnp.transpose(v.reshape(4, ROWS, FRAMES, COLS), (0, 2, 1, 3))

time: 55.9 us -> 51.8 us (0.927)
  Pallas kernels: 52 us -> 49.8 us
  other arithmetic: 1.56 us -> 0.66 us
  local copies, waits for them, and re-layouts: 1.54 us -> 0.64 us
    pallas_call x1, Pallas kernels: 52 us -> 49.8 us  [per_device(): pl.pallas_call(functools.partial(kernel, nq, ns), out_shape=(jax.ShapeDty...]
    unnamed x3, local copies, waits for them, and re-layouts: 1.54 us -> 0.64 us
    broadcast_in_dim x1, other arithmetic: 1.56 us -> 0.66 us  [per_device(): return (as_frames(noise)[None], next_queue[None])]
where the time goes in v2:
time: 51.8 us; the launch traced here: 51.7 us
  Pallas kernels  49.8 us (96%)
  between operations  0.67 us (1%)
  other arithmetic  0.66 us (1%)
  local copies, waits for them, and re-layouts  0.64 us (1%)
    pallas_call x1, Pallas kernels, per_device(): pl.pallas_call(functools.partial(kernel, nq, ns), out_shape=(jax.ShapeDty...  49.8 us

profile of v2, /device:TPU:1, one launch (start us, length us, event | category | flops | bytes accessed | tf_op | source)
XLA Modules:
  0.0 51.7 jit_solution(12510795626007159922)
XLA Ops:
  0.6 0.0 copy-start
  0.7 49.8 %shard_map.140 = (f32[192,16]{1,0:T(8,128)S(1)}, f32[192,16]{1,0:T(8,128)S(1)}) custom-call(s32[16]{0:T(128)} %ts_hbm.1, s32[16]{0:T(128)} %map_hbm.1, f32[192,16]{1,0:T(8,128)} %bitcast.20, bf16[3,3,4,320]{3,2,1,0:T(4,128)(2,1)} %cin_hbm.1, bf16[320,1280]{1,0:T(8,128)(2,1)} %tw1_hbm.1, bf16[1280,1280]{1,0:T(8,128)(2,1)} %tw2_hbm.1, ...), custom_call_target="tpu_custom_call" | custom-call | flops 10000000000 | bytes 10000000 | tf_op jit(solution)/shard_map/pallas_call | solution.py:581
  50.4 0.0 copy-done
  50.4 0.7 %select_bitcast_fusion = f32[1,4,16,3,16]{4,2,3,1,0:T(8,128)} fusion(f32[4,16,3,16]{3,1,2,0:T(8,128)S(1)} %copy-done, f32[4,16,3,16]{3,1,2,0:T(8,128)S(1)} %bitcast.18, pred[]{:T(512)S(6)} %eq.3), kind=kLoop, calls=%fused_computation | loop fusion | flops 3072 | bytes 36865 | tf_op jit(solution)/shard_map/broadcast_in_dim | solution.py:641
  51.1 0.6 %copy.16 = f32[1,4,16,3,16]{4,2,3,1,0:T(8,128)} copy(f32[1,4,16,3,16]{4,2,3,1,0:T(8,128)S(1)} %bitcast.17) | data formatting | bytes 24576
Async XLA Ops:
  0.6 49.8 %copy-start = (f32[4,16,3,16]{3,1,2,0:T(8,128)S(1)}, f32[4,16,3,16]{3,1,2,0:T(8,128)}, u32[]{:S(2)}) copy-start(f32[4,16,3,16]{3,1,2,0:T(8,128)} %param.14) | copy-start | bytes 36868

commit v3 on v2

--- a/solution.py
+++ b/solution.py
@@ -48,6 +48,11 @@
     left = v - hi.astype(F32)
     mid = left.astype(BF)
     return hi, mid, (left - mid.astype(F32)).astype(BF)
+
+
+def stack(parts):
+    rows = [p.astype(F32) for p in parts]
+    return jnp.concatenate(rows + [jnp.zeros((16 - len(rows), rows[0].shape[1]), F32)], axis=0).astype(BF)
 
 
 def kernel(
@@ -82,7 +87,7 @@
     load_sem,
     lat_f,
     lat_b,
-    xt,
+    shifted,
     cin_f,
     cin_w,
     stream,
@@ -128,6 +133,9 @@
     first = s == 0
     last = s == ns - 1
 
+    def cells(r, n=1):
+        return pl.ds(r * CELLS if isinstance(r, int) else pl.multiple_of(r * CELLS, CELLS), n * CELLS)
+
     barrier = pltpu.get_barrier_semaphore()
 
     def greet(j, _):
@@ -163,21 +171,29 @@
     load_lat, load_cin, load_tw1, load_tw2, load_emb, load_c1, load_c2, load_qkv, load_proj, load_cout, load_ts, load_map = loads
 
     load_lat.wait()
-    lat_f[12:16, :] = jnp.zeros((4, CELLS), F32)
+    lat_f[12:16, :] = jnp.where(iota((4, CELLS), 0) == 0, 1.0, 0.0)
     for f in range(FRAMES):
         lat_f[0:12, f * COLS : (f + 1) * COLS] = lat_v[pl.ds(f, 12, stride=FRAMES), :]
-    lat_b[1] = lat_f[...].astype(BF)
+    own_rows = pl.ds(pl.multiple_of((s + 1) * 16, 16), 16)
+    lat_b[own_rows, :] = lat_f[...].astype(BF)
+    lat_b[0:16, :] = jnp.zeros((16, CELLS), BF)
+    lat_b[(ns + 1) * 16 :, :] = jnp.zeros((16, CELLS), BF)
 
     pl.semaphore_wait(barrier, ns - 1 + 3)
 
-    lat_down = pltpu.make_async_remote_copy(
-        lat_b.at[1], lat_b.at[0], lat_send.at[0], lat_recv.at[0], device_id=(q, down), device_id_type=MESH
-    )
-    lat_up = pltpu.make_async_remote_copy(
-        lat_b.at[1], lat_b.at[2], lat_send.at[1], lat_recv.at[1], device_id=(q, up), device_id_type=MESH
-    )
-    lat_down.start()
-    lat_up.start()
+    lat_sends = {
+        j: pltpu.make_async_remote_copy(
+            lat_b.at[own_rows],
+            lat_b.at[own_rows],
+            lat_send,
+            lat_recv.at[0 if j == 1 else 1 if j == ns - 1 else 2],
+            device_id=(q, lax.rem(s + j, ns)),
+            device_id_type=MESH,
+        )
+        for j in order
+    }
+    for j in order:
+        lat_sends[j].start()
 
     ci = iota((CH, CH), 0) * 6554 >> 16
     cj = iota((CH, CH), 1) * 6554 >> 16
@@ -190,18 +206,17 @@
             t = a * 3 + b
             cin_f[t * 4 : t * 4 + 4, :] = cin_v[a, b].astype(F32)
 
-    kk = iota((128, 40), 0)
-    jj = iota((128, 40), 1)
-    tap_b = jnp.where(kk >= 36, 1, 0) + jnp.where(kk >= 72, 1, 0)
-    left = kk - 36 * tap_b
-    part = left * 5462 >> 16
-    left = left - 12 * part
-    chan = left * 21846 >> 16
-    row_of = 3 * part + left - 3 * chan
+    kk = iota((144, 40), 0)
+    jj = iota((144, 40), 1)
+    tap_b = jnp.where(kk >= 48, 1, 0) + jnp.where(kk >= 96, 1, 0)
+    left = kk - 48 * tap_b
+    in_block = left & 15
+    chan = in_block * 21846 >> 16
+    row_of = 3 * (left >> 4) + in_block - 3 * chan
 
     def place_cin(y, _):
         tap_a = row_of - y
-        hit = (tap_a >= 0) & (tap_a < 3) & (jj == (tap_a * 3 + tap_b) * 4 + chan)
+        hit = (tap_a >= 0) & (tap_a < 3) & (in_block < 12) & (jj == (tap_a * 3 + tap_b) * 4 + chan)
         sel = jnp.where(hit, 1.0, 0.0).astype(BF)
         cin_w[y] = dot(sel, cin_f[...].astype(BF)).astype(BF)
         return 0
@@ -224,27 +239,22 @@
         nr[which, :, 3 * REST : 256] = jnp.zeros((1024, 256 - 3 * REST), BF)
         nr[which, 768 + 3 * REST : 1024, :] = jnp.zeros((256 - 3 * REST, 256), BF)
 
-    lat_down.wait_recv()
-    lat_up.wait_recv()
-    lane = iota((16, CELLS), 1) & (COLS - 1)
-    xt[108:128, :] = jnp.zeros((20, CELLS), F32)
-    for n in range(3):
-        v = lat_b[n].astype(F32)
-        if n == 0:
-            v = jnp.where(first, 0.0, v)
-        if n == 2:
-            v = jnp.where(last, 0.0, v)
-        shifted = (
-            jnp.where(lane == 0, 0.0, pltpu.roll(v, 1, 1)),
-            v,
-            jnp.where(lane == COLS - 1, 0.0, pltpu.roll(v, CELLS - 1, 1)),
-        )
-        for b in range(3):
-            xt[b * 36 + n * 12 : b * 36 + n * 12 + 12, :] = shifted[b][0:12]
-    x_in = xt[...].T.astype(BF)
-
-    def cells(r, n=1):
-        return pl.ds(r * CELLS if isinstance(r, int) else pl.multiple_of(r * CELLS, CELLS), n * CELLS)
+    def shift_blocks(start, n):
+        rows = pl.ds(start if isinstance(start, int) else pl.multiple_of(start * 16, 16), n * 16)
+        v = lat_b[rows, :].astype(F32)
+        lane = iota((n * 16, CELLS), 1) & (COLS - 1)
+        shifted[0, rows, :] = jnp.where(lane == 0, 0.0, pltpu.roll(v, 1, 1)).astype(BF)
+        shifted[1, rows, :] = lat_b[rows, :]
+        shifted[2, rows, :] = jnp.where(lane == COLS - 1, 0.0, pltpu.roll(v, CELLS - 1, 1)).astype(BF)
+
+    lat_sends[1].wait_recv()
+    lat_sends[ns - 1].wait_recv()
+    shift_blocks(s, 3)
+    window = pl.ds(pl.multiple_of(s * 16, 16), 48)
+    x_in = jnp.concatenate([shifted[b, window, :] for b in range(3)], axis=0).astype(F32).T.astype(BF)
+
+    for y in range(7):
+        stream[cells(y), :] = dot(x_in, cin_w[y])
 
     def row_stats(r, x):
         m = jnp.sum(x, axis=0, keepdims=True) * (1.0 / CELLS)
@@ -269,19 +279,18 @@
         near = dot(jnp.broadcast_to(mean, (16, CH)).astype(BF), pairs[...])
         return near[0:1] * (1.0 / PER_GROUP)
 
-    def take_stats(phase, near):
+    def take_stats(phase, near, shift=0.0):
         pltpu.make_async_copy(
             stats.at[phase, pl.ds(0, ns - 1)], stats.at[phase, pl.ds(0, ns - 1)], stat_recv.at[phase]
         ).wait()
         v = stats[phase]
-        d = v - jnp.concatenate([near, jnp.zeros_like(near)], axis=0)
+        d = v - jnp.concatenate([near - shift, jnp.zeros_like(near)], axis=0)
         total = jnp.sum(d, axis=0)
         square = jnp.sum(d * d, axis=0)
         s1 = total[0:1]
         s2 = total[1:2] + (ROWS * CELLS) * square[0:1]
         parts = split3(s1) + split3(s2)
-        stacked = jnp.concatenate([p.astype(F32) for p in parts] + [jnp.zeros((10, CH), F32)], axis=0)
-        g = dot(stacked.astype(BF), pairs[...])
+        g = dot(stack(parts), pairs[...])
         off = (g[0:1] + g[1:2] + g[2:3]) * (1.0 / (ns * PER_GROUP))
         spread = (g[3:4] + g[4:5] + g[5:6]) * (1.0 / (ns * PER_GROUP * ROWS * CELLS)) - off * off
         return near + off, lax.rsqrt(jnp.maximum(spread, 0.0) + NORM_EPS)
@@ -330,20 +339,52 @@
         )
         return main, rest
 
-    def stream_row(y):
-        v = dot(x_in, cin_w[y])
-        stream[cells(y), :] = v
-        return v
-
-    def own_stream(i, _):
-        row_stats(i, stream_row(i + 2))
+    load_c1.wait()
+    shared_passes(0, c1_v)
+
+    pltpu.make_async_copy(lat_b.at[pl.ds(0, (ns - 3) * 16)], lat_b.at[pl.ds(0, (ns - 3) * 16)], lat_recv.at[2]).wait()
+    shift_blocks(0, ns + 2)
+    every = jnp.concatenate(
+        [jnp.concatenate([shifted[b, n * 16 : n * 16 + 48, :] for b in range(3)], axis=0) for n in range(ns)], axis=1
+    )
+    products = jnp.concatenate(split3(dot_nt(every, every)), axis=0)
+    first_sum = jnp.zeros((1, CH), F32)
+    second_sum = jnp.zeros((1, CH), F32)
+    for y in (2, 3, 4):
+        w = cin_w[y]
+        g = dot(products, w)
+        g = g[0:144] + g[144:288] + g[288:432]
+        first_sum = first_sum + g[76:77]
+        second_sum = second_sum + jnp.sum(w.astype(F32) * g, axis=0, keepdims=True)
+    per_cell = 1.0 / (ns * ROWS * CELLS * PER_GROUP)
+    g = dot(stack(split3(first_sum) + split3(second_sum)), pairs[...])
+    mean = (g[0:1] + g[1:2] + g[2:3]) * per_cell
+    spread = (g[3:4] + g[4:5] + g[5:6]) * per_cell - mean * mean
+    inv = lax.rsqrt(jnp.maximum(spread, 0.0) + NORM_EPS)
+    half_inv = 0.5 * inv
+
+    def norm1(r, _):
+        y = silu_of_half((stream[cells(r), :] - mean) * half_inv)
+        row = s * ROWS + r - 2
+        put_normed(r, jnp.where((row >= 0) & (row < ns * ROWS), y, 0.0))
         return 0
 
-    lax.fori_loop(0, ROWS, own_stream, 0)
-    near1 = send_stats(0)
-
-    for y in (0, 1, 5, 6):
-        stream_row(y)
+    lax.fori_loop(1, 6, norm1, 0)
+
+    def hidden_rows(rows):
+        main, rest = conv_rows(0, c1_v, rows)
+        for i, j in enumerate(rows):
+            hidden[cells(j), 0:MAIN] = main[i * CELLS : (i + 1) * CELLS]
+            hidden[cells(j), MAIN:CH] = rest[i * CELLS : (i + 1) * CELLS]
+
+    hidden_rows((1, 2, 3))
+    for i in range(ROWS):
+        row_stats(i, hidden[cells(i + 1), :])
+    near2 = send_stats(0)
+
+    norm1(0, 0)
+    norm1(6, 0)
+    hidden_rows((0, 4))
 
     load_ts.wait()
     load_map.wait()
@@ -361,38 +402,11 @@
     second = silu_of_half(0.5 * h).astype(BF)
     load_emb.wait()
     bias[...] = dot_nt(second, emb_v[...])[0:1]
-    load_c1.wait()
-    shared_passes(0, c1_v)
-
-    mean, inv = take_stats(0, near1)
-    half_inv = 0.5 * inv
-
-    def norm1(r, _):
-        y = silu_of_half((stream[cells(r), :] - mean) * half_inv)
-        row = s * ROWS + r - 2
-        put_normed(r, jnp.where((row >= 0) & (row < ns * ROWS), y, 0.0))
-        return 0
-
-    lax.fori_loop(1, 6, norm1, 0)
-
-    def hidden_rows(rows):
-        main, rest = conv_rows(0, c1_v, rows)
-        for i, j in enumerate(rows):
-            hidden[cells(j), 0:MAIN] = main[i * CELLS : (i + 1) * CELLS] + bias[:, 0:MAIN]
-            hidden[cells(j), MAIN:CH] = rest[i * CELLS : (i + 1) * CELLS] + bias[:, MAIN:CH]
-
-    hidden_rows((1, 2, 3))
-    for i in range(ROWS):
-        row_stats(i, hidden[cells(i + 1), :])
-    near2 = send_stats(1)
-
-    norm1(0, 0)
-    norm1(6, 0)
-    hidden_rows((0, 4))
     load_c2.wait()
     shared_passes(1, c2_v)
 
-    mean2, inv2 = take_stats(1, near2)
+    mean2, inv2 = take_stats(0, near2, bias[...])
+    mean2 = mean2 - bias[...]
     half_inv2 = 0.5 * inv2
 
     def norm2(r, _):
@@ -408,7 +422,7 @@
     block[:, MAIN:CH] = stream[cells(2, ROWS), MAIN:CH] + rest
     for i in range(ROWS):
         row_stats(i, block[cells(i), :])
-    near3 = send_stats(2)
+    near3 = send_stats(1)
 
     load_qkv.wait()
     wqkv[:, 0:CH] = qkv_v[:, 0:CH] * jnp.asarray(HEAD_DIM**-0.5, BF)
@@ -452,7 +466,7 @@
     keep = jnp.sqrt(alpha_next / alpha_now)
     gain = jnp.sqrt(1.0 - alpha_next) - keep * jnp.sqrt(1.0 - alpha_now)
 
-    mean3, inv3 = take_stats(2, near3)
+    mean3, inv3 = take_stats(1, near3)
 
     same = ((iota((CELLS, CELLS), 0) ^ iota((CELLS, CELLS), 1)) & (COLS - 1)) == 0
     low_half = iota((CELLS, 128), 1) < HEAD_DIM
@@ -483,8 +497,8 @@
     block[...] += dot(attended[...], wproj[...])
     for i in range(ROWS):
         row_stats(i, block[cells(i), :])
-    near4 = send_stats(3)
-    mean4, inv4 = take_stats(3, near4)
+    near4 = send_stats(2)
+    mean4, inv4 = take_stats(2, near4)
     half_inv4 = 0.5 * inv4
 
     z = jnp.zeros((144, CELLS), F32)
@@ -542,9 +556,8 @@
     sends[2].wait_recv()
     put(next_ref, main_in[...] + jnp.where(first, 0.0, edge_next[0]) + jnp.where(last, 0.0, edge_next[1]))
 
-    lat_down.wait_send()
-    lat_up.wait_send()
-    for phase in range(4):
+    pltpu.make_async_copy(lat_b.at[pl.ds(0, (ns - 1) * 16)], lat_b.at[pl.ds(0, (ns - 1) * 16)], lat_send).wait()
+    for phase in range(3):
         stats_sent(phase)
     for send in sends:
         send.wait_send()
@@ -592,10 +605,10 @@
         + [
             DMA((len(operands),)),
             pltpu.VMEM((16, CELLS), F32),
-            pltpu.VMEM((3, 16, CELLS), BF),
-            pltpu.VMEM((128, CELLS), F32),
+            pltpu.VMEM(((ns + 2) * 16, CELLS), BF),
+            pltpu.VMEM((3, (ns + 2) * 16, CELLS), BF),
             pltpu.VMEM((40, CH), F32),
-            pltpu.VMEM((7, 128, CH), BF),
+            pltpu.VMEM((7, 144, CH), BF),
             pltpu.VMEM((7 * CELLS, CH), F32),
             pltpu.VMEM((5 * CELLS, CH), F32),
             pltpu.VMEM((3 * CELLS, CH), F32),
@@ -612,17 +625,17 @@
             pltpu.VMEM((3, 144, CH), BF),
             pltpu.VMEM((ROWS * CELLS, 384), BF),
             pltpu.VMEM((2, 8, CH), F32),
-            pltpu.VMEM((4, ns, 2, CH), F32),
+            pltpu.VMEM((3, ns, 2, CH), F32),
             pltpu.VMEM((2, 16, CELLS), F32),
             pltpu.VMEM((2, 16, CELLS), F32),
             pltpu.VMEM((2, 16, CELLS), F32),
             pltpu.VMEM((2, 16, CELLS), F32),
             pltpu.VMEM((16, CELLS), F32),
             pltpu.VMEM((16, CELLS), F32),
-            DMA((2,)),
-            DMA((2,)),
-            DMA((4,)),
-            DMA((4,)),
+            DMA,
+            DMA((3,)),
+            DMA((3,)),
+            DMA((3,)),
             DMA((4,)),
             DMA((4,)),
             DMA,

time: 51.8 us -> 49.2 us (0.950)
  Pallas kernels: 49.8 us -> 47 us
    pallas_call x1, Pallas kernels: 49.8 us -> 47 us  [per_device(): pl.pallas_call(functools.partial(kernel, nq, ns), out_shape=(jax.ShapeDty...]
where the time goes in v3:
time: 49.2 us; the launch traced here: 48.9 us
  Pallas kernels  47 us (96%)
  between operations  0.67 us (1%)
  other arithmetic  0.66 us (1%)
  local copies, waits for them, and re-layouts  0.64 us (1%)
    pallas_call x1, Pallas kernels, per_device(): pl.pallas_call(functools.partial(kernel, nq, ns), out_shape=(jax.ShapeDty...  47 us

profile of v3, /device:TPU:1, one launch (start us, length us, event | category | flops | bytes accessed | tf_op | source)
XLA Modules:
  0.0 48.9 jit_solution(12417430484539199236)
XLA Ops:
  0.6 0.0 copy-start
  0.7 47.0 %shard_map.140 = (f32[192,16]{1,0:T(8,128)S(1)}, f32[192,16]{1,0:T(8,128)S(1)}) custom-call(s32[16]{0:T(128)} %ts_hbm.1, s32[16]{0:T(128)} %map_hbm.1, f32[192,16]{1,0:T(8,128)} %bitcast.20, bf16[3,3,4,320]{3,2,1,0:T(4,128)(2,1)} %cin_hbm.1, bf16[320,1280]{1,0:T(8,128)(2,1)} %tw1_hbm.1, bf16[1280,1280]{1,0:T(8,128)(2,1)} %tw2_hbm.1, ...), custom_call_target="tpu_custom_call" | custom-call | flops 10000000000 | bytes 10000000 | tf_op jit(solution)/shard_map/pallas_call | solution.py:594
  47.6 0.0 copy-done
  47.6 0.7 %select_bitcast_fusion = f32[1,4,16,3,16]{4,2,3,1,0:T(8,128)} fusion(f32[4,16,3,16]{3,1,2,0:T(8,128)S(1)} %copy-done, f32[4,16,3,16]{3,1,2,0:T(8,128)S(1)} %bitcast.18, pred[]{:T(512)S(6)} %eq.3), kind=kLoop, calls=%fused_computation | loop fusion | flops 3072 | bytes 36865 | tf_op jit(solution)/shard_map/broadcast_in_dim | solution.py:654
  48.3 0.6 %copy.16 = f32[1,4,16,3,16]{4,2,3,1,0:T(8,128)} copy(f32[1,4,16,3,16]{4,2,3,1,0:T(8,128)S(1)} %bitcast.17) | data formatting | bytes 24576
Async XLA Ops:
  0.6 47.0 %copy-start = (f32[4,16,3,16]{3,1,2,0:T(8,128)S(1)}, f32[4,16,3,16]{3,1,2,0:T(8,128)}, u32[]{:S(2)}) copy-start(f32[4,16,3,16]{3,1,2,0:T(8,128)} %param.14) | copy-start | bytes 36868

commit v4 on v3

--- a/solution.py
+++ b/solution.py
@@ -107,31 +107,21 @@
     attended,
     rows_st,
     stats,
-    edge_raw,
-    edge_scaled,
-    edge_in,
-    edge_next,
     main_out,
     main_in,
     lat_send,
     lat_recv,
     stat_send,
     stat_recv,
-    edge_send,
-    edge_recv,
     main_send,
     main_recv,
 ):
     q = lax.axis_index("queue")
     s = lax.axis_index("space")
-    up = lax.rem(s + ns - 1, ns)
-    down = lax.rem(s + 1, ns)
     ahead = lax.rem(q + 1, nq)
     behind = lax.rem(q + nq - 1, nq)
     ring = ns // 2
     order = sorted(range(1, ns), key=lambda j: -min(j % ring, ring - j % ring))
-    first = s == 0
-    last = s == ns - 1
 
     def cells(r, n=1):
         return pl.ds(r * CELLS if isinstance(r, int) else pl.multiple_of(r * CELLS, CELLS), n * CELLS)
@@ -144,8 +134,7 @@
         return 0
 
     lax.fori_loop(1, ns, greet, 0)
-    for peer in (up, s, down):
-        pl.semaphore_signal(barrier, inc=1, device_id=(behind, peer), device_id_type=MESH)
+    pl.semaphore_signal(barrier, inc=1, device_id=(behind, s), device_id_type=MESH)
 
     loads = [
         pltpu.make_async_copy(src, dst, load_sem.at[i])
@@ -174,19 +163,19 @@
     lat_f[12:16, :] = jnp.where(iota((4, CELLS), 0) == 0, 1.0, 0.0)
     for f in range(FRAMES):
         lat_f[0:12, f * COLS : (f + 1) * COLS] = lat_v[pl.ds(f, 12, stride=FRAMES), :]
-    own_rows = pl.ds(pl.multiple_of((s + 1) * 16, 16), 16)
+    own_rows = pl.ds(pl.multiple_of((s + 2) * 16, 16), 16)
     lat_b[own_rows, :] = lat_f[...].astype(BF)
-    lat_b[0:16, :] = jnp.zeros((16, CELLS), BF)
-    lat_b[(ns + 1) * 16 :, :] = jnp.zeros((16, CELLS), BF)
-
-    pl.semaphore_wait(barrier, ns - 1 + 3)
+    lat_b[0:32, :] = jnp.zeros((32, CELLS), BF)
+    lat_b[(ns + 2) * 16 :, :] = jnp.zeros((32, CELLS), BF)
+
+    pl.semaphore_wait(barrier, ns - 1 + 1)
 
     lat_sends = {
         j: pltpu.make_async_remote_copy(
             lat_b.at[own_rows],
             lat_b.at[own_rows],
             lat_send,
-            lat_recv.at[0 if j == 1 else 1 if j == ns - 1 else 2],
+            lat_recv.at[(1, 2, ns - 2, ns - 1).index(j) if j in (1, 2, ns - 2, ns - 1) else 4],
             device_id=(q, lax.rem(s + j, ns)),
             device_id_type=MESH,
         )
@@ -195,6 +184,22 @@
     for j in order:
         lat_sends[j].start()
 
+    load_ts.wait()
+    load_map.wait()
+    level = ts_ref[map_ref[q]]
+    pos = iota((16, CH), 1)
+    half = CH // 2
+    k = jnp.where(pos < half, pos, pos - half).astype(F32)
+    phases = level.astype(F32) * jnp.exp(k * (-math.log(10000.0) / half))
+    sinusoid = jnp.where(pos < half, jnp.cos(phases), jnp.sin(phases)).astype(BF)
+    load_tw1.wait()
+    h = dot(sinusoid, tw1_v[...])
+    first_hidden = silu_of_half(0.5 * h).astype(BF)
+    load_tw2.wait()
+    h = dot(first_hidden, tw2_v[...])
+    second = silu_of_half(0.5 * h).astype(BF)
+    load_emb.wait()
+    bias[...] = dot_nt(second, emb_v[...])[0:1]
     ci = iota((CH, CH), 0) * 6554 >> 16
     cj = iota((CH, CH), 1) * 6554 >> 16
     pairs[...] = jnp.where(ci == cj, 1.0, 0.0).astype(BF)
@@ -223,7 +228,7 @@
 
     lax.fori_loop(0, 7, place_cin, 0)
 
-    xr[:, 192:256] = jnp.zeros((9 * CELLS, 64), BF)
+    xr[:, 192:256] = jnp.zeros((11 * CELLS, 64), BF)
 
     def shared_passes(which, w):
         for b in range(3):
@@ -240,21 +245,26 @@
         nr[which, 768 + 3 * REST : 1024, :] = jnp.zeros((256 - 3 * REST, 256), BF)
 
     def shift_blocks(start, n):
-        rows = pl.ds(start if isinstance(start, int) else pl.multiple_of(start * 16, 16), n * 16)
+        rows = pl.ds(start * 16 if isinstance(start, int) else pl.multiple_of(start * 16, 16), n * 16)
         v = lat_b[rows, :].astype(F32)
         lane = iota((n * 16, CELLS), 1) & (COLS - 1)
         shifted[0, rows, :] = jnp.where(lane == 0, 0.0, pltpu.roll(v, 1, 1)).astype(BF)
         shifted[1, rows, :] = lat_b[rows, :]
         shifted[2, rows, :] = jnp.where(lane == COLS - 1, 0.0, pltpu.roll(v, CELLS - 1, 1)).astype(BF)
 
-    lat_sends[1].wait_recv()
-    lat_sends[ns - 1].wait_recv()
-    shift_blocks(s, 3)
-    window = pl.ds(pl.multiple_of(s * 16, 16), 48)
-    x_in = jnp.concatenate([shifted[b, window, :] for b in range(3)], axis=0).astype(F32).T.astype(BF)
-
+    for j in (1, 2, ns - 2, ns - 1):
+        lat_sends[j].wait_recv()
+    shift_blocks(s, 5)
+
+    def cells_of(slot):
+        window = pl.ds(pl.multiple_of(slot * 16, 16), 48)
+        return jnp.concatenate([shifted[b, window, :] for b in range(3)], axis=0).astype(F32).T.astype(BF)
+
+    x_in = cells_of(s + 1)
     for y in range(7):
-        stream[cells(y), :] = dot(x_in, cin_w[y])
+        stream[cells(y + 1), :] = dot(x_in, cin_w[y])
+    stream[cells(0), :] = dot(cells_of(s), cin_w[2])
+    stream[cells(8), :] = dot(cells_of(s + 2), cin_w[4])
 
     def row_stats(r, x):
         m = jnp.sum(x, axis=0, keepdims=True) * (1.0 / CELLS)
@@ -342,10 +352,10 @@
     load_c1.wait()
     shared_passes(0, c1_v)
 
-    pltpu.make_async_copy(lat_b.at[pl.ds(0, (ns - 3) * 16)], lat_b.at[pl.ds(0, (ns - 3) * 16)], lat_recv.at[2]).wait()
-    shift_blocks(0, ns + 2)
+    pltpu.make_async_copy(lat_b.at[pl.ds(0, (ns - 5) * 16)], lat_b.at[pl.ds(0, (ns - 5) * 16)], lat_recv.at[4]).wait()
+    shift_blocks(1, ns + 2)
     every = jnp.concatenate(
-        [jnp.concatenate([shifted[b, n * 16 : n * 16 + 48, :] for b in range(3)], axis=0) for n in range(ns)], axis=1
+        [jnp.concatenate([shifted[b, n * 16 + 16 : n * 16 + 64, :] for b in range(3)], axis=0) for n in range(ns)], axis=1
     )
     products = jnp.concatenate(split3(dot_nt(every, every)), axis=0)
     first_sum = jnp.zeros((1, CH), F32)
@@ -363,13 +373,15 @@
     inv = lax.rsqrt(jnp.maximum(spread, 0.0) + NORM_EPS)
     half_inv = 0.5 * inv
 
+    def normed(r, x, mean, half_inv, row):
+        inside = jnp.where((s * ROWS + row >= 0) & (s * ROWS + row < ns * ROWS), half_inv, 0.0)
+        put_normed(r, silu_of_half((x - mean) * inside))
+
     def norm1(r, _):
-        y = silu_of_half((stream[cells(r), :] - mean) * half_inv)
-        row = s * ROWS + r - 2
-        put_normed(r, jnp.where((row >= 0) & (row < ns * ROWS), y, 0.0))
+        normed(r, stream[cells(r), :], mean, half_inv, r - 3)
         return 0
 
-    lax.fori_loop(1, 6, norm1, 0)
+    lax.fori_loop(2, 7, norm1, 0)
 
     def hidden_rows(rows):
         main, rest = conv_rows(0, c1_v, rows)
@@ -377,31 +389,14 @@
             hidden[cells(j), 0:MAIN] = main[i * CELLS : (i + 1) * CELLS]
             hidden[cells(j), MAIN:CH] = rest[i * CELLS : (i + 1) * CELLS]
 
-    hidden_rows((1, 2, 3))
+    hidden_rows((2, 3, 4))
     for i in range(ROWS):
-        row_stats(i, hidden[cells(i + 1), :])
+        row_stats(i, hidden[cells(i + 2), :])
     near2 = send_stats(0)
 
-    norm1(0, 0)
-    norm1(6, 0)
-    hidden_rows((0, 4))
-
-    load_ts.wait()
-    load_map.wait()
-    level = ts_ref[map_ref[q]]
-    pos = iota((16, CH), 1)
-    half = CH // 2
-    k = jnp.where(pos < half, pos, pos - half).astype(F32)
-    phases = level.astype(F32) * jnp.exp(k * (-math.log(10000.0) / half))
-    sinusoid = jnp.where(pos < half, jnp.cos(phases), jnp.sin(phases)).astype(BF)
-    load_tw1.wait()
-    h = dot(sinusoid, tw1_v[...])
-    first_hidden = silu_of_half(0.5 * h).astype(BF)
-    load_tw2.wait()
-    h = dot(first_hidden, tw2_v[...])
-    second = silu_of_half(0.5 * h).astype(BF)
-    load_emb.wait()
-    bias[...] = dot_nt(second, emb_v[...])[0:1]
+    lax.fori_loop(0, 2, norm1, 0)
+    lax.fori_loop(7, 9, norm1, 0)
+    hidden_rows((0, 1, 5, 6))
     load_c2.wait()
     shared_passes(1, c2_v)
 
@@ -410,19 +405,25 @@
     half_inv2 = 0.5 * inv2
 
     def norm2(r, _):
-        y = silu_of_half((hidden[cells(r), :] - mean2) * half_inv2)
-        row = s * ROWS + r - 1
-        put_normed(r, jnp.where((row >= 0) & (row < ns * ROWS), y, 0.0))
+        normed(r, hidden[cells(r), :], mean2, half_inv2, r - 2)
         return 0
 
-    lax.fori_loop(0, 5, norm2, 0)
-
-    main, rest = conv_rows(1, c2_v, (0, 1, 2))
-    block[:, 0:MAIN] = stream[cells(2, ROWS), 0:MAIN] + main
-    block[:, MAIN:CH] = stream[cells(2, ROWS), MAIN:CH] + rest
+    lax.fori_loop(1, 6, norm2, 0)
+
+    def block_rows(rows):
+        main, rest = conv_rows(1, c2_v, rows)
+        for i, j in enumerate(rows):
+            block[cells(j), 0:MAIN] = stream[cells(j + 2), 0:MAIN] + main[i * CELLS : (i + 1) * CELLS]
+            block[cells(j), MAIN:CH] = stream[cells(j + 2), MAIN:CH] + rest[i * CELLS : (i + 1) * CELLS]
+
+    block_rows((1, 2, 3))
     for i in range(ROWS):
-        row_stats(i, block[cells(i), :])
+        row_stats(i, block[cells(i + 1), :])
     near3 = send_stats(1)
+
+    norm2(0, 0)
+    norm2(6, 0)
+    block_rows((0, 4))
 
     load_qkv.wait()
     wqkv[:, 0:CH] = qkv_v[:, 0:CH] * jnp.asarray(HEAD_DIM**-0.5, BF)
@@ -437,15 +438,13 @@
         for b in range(3):
             r = (a * 3 + b) * 4
             cout_f[r : r + 4, :] = cout_v[a, b].astype(F32)
-    to = iota((144, 40), 0)
-    src = iota((144, 40), 1)
-    to_b = jnp.where(to >= 48, 1, 0) + jnp.where(to >= 96, 1, 0)
-    to_part = to - 48 * to_b >> 4
+    to = iota((48, 40), 0)
+    src = iota((48, 40), 1)
+    to_b = to >> 4
     to_row = to & 15
     to_c = to_row * 21846 >> 16
-    to_y = to_row - 3 * to_c + jnp.where(to_part == 1, ROWS, 0) - jnp.where(to_part == 2, ROWS, 0)
-    for i in range(ROWS):
-        tap = i - to_y + 1
+    for i in range(ROWS + 2):
+        tap = i - (to_row - 3 * to_c)
         hit = (tap >= 0) & (tap < 3) & (to_row < 12) & (src == (tap * 3 + to_b) * 4 + to_c)
         wout[i] = dot(jnp.where(hit, 1.0, 0.0).astype(BF), cout_f[...].astype(BF)).astype(BF)
 
@@ -471,7 +470,14 @@
     same = ((iota((CELLS, CELLS), 0) ^ iota((CELLS, CELLS), 1)) & (COLS - 1)) == 0
     low_half = iota((CELLS, 128), 1) < HEAD_DIM
 
-    projected[...] = dot(((block[...] - mean3) * inv3).astype(BF), wqkv[...]).astype(BF)
+    def project(rows):
+        projected[rows, :] = dot(((block[rows, :] - mean3) * inv3).astype(BF), wqkv[...]).astype(BF)
+
+    def mix(rows):
+        block[rows, :] += dot(attended[rows, :], wproj[...])
+
+    own_cells = cells(1, ROWS)
+    project(own_cells)
 
     def attend_row(i, _):
         row = cells(i)
@@ -493,52 +499,37 @@
         attended[row, 256:384] = jnp.where(low_half, head(3), head(4)).astype(BF)
         return 0
 
-    lax.fori_loop(0, ROWS, attend_row, 0)
-    block[...] += dot(attended[...], wproj[...])
+    lax.fori_loop(1, ROWS + 1, attend_row, 0)
+    mix(own_cells)
     for i in range(ROWS):
-        row_stats(i, block[cells(i), :])
+        row_stats(i, block[cells(i + 1), :])
     near4 = send_stats(2)
+
+    for i in (0, ROWS + 1):
+        project(cells(i))
+
+    def attend_halo(i, _):
+        return attend_row(i * (ROWS + 1), 0)
+
+    lax.fori_loop(0, 2, attend_halo, 0)
+    for i in (0, ROWS + 1):
+        mix(cells(i))
+
     mean4, inv4 = take_stats(2, near4)
     half_inv4 = 0.5 * inv4
 
-    z = jnp.zeros((144, CELLS), F32)
-    for i in range(ROWS):
-        z = z + dot_nt(wout[i], silu_of_half((block[cells(i), :] - mean4) * half_inv4).astype(BF))
-    lane = iota((48, CELLS), 1) & (COLS - 1)
-    sums = (
-        z[48:96]
-        + jnp.where(lane == 0, 0.0, pltpu.roll(z[0:48], 1, 1))
-        + jnp.where(lane == COLS - 1, 0.0, pltpu.roll(z[96:144], CELLS - 1, 1))
+    z = jnp.zeros((48, CELLS), F32)
+    for i in range(ROWS + 2):
+        row = s * ROWS + i - 1
+        inside = jnp.where((row >= 0) & (row < ns * ROWS), half_inv4, 0.0)
+        z = z + dot_nt(wout[i], silu_of_half((block[cells(i), :] - mean4) * inside).astype(BF))
+    lane = iota((16, CELLS), 1) & (COLS - 1)
+    noise = (
+        z[16:32]
+        + jnp.where(lane == 0, 0.0, pltpu.roll(z[0:16], 1, 1))
+        + jnp.where(lane == COLS - 1, 0.0, pltpu.roll(z[32:48], CELLS - 1, 1))
     )
-    own = sums[0:16]
-    for side in range(2):
-        edge_raw[side] = sums[16 + 16 * side : 32 + 16 * side]
-        edge_scaled[side] = gain * sums[16 + 16 * side : 32 + 16 * side]
-    sends = []
-    for side, peer in ((0, down), (1, up)):
-        sends.append(
-            pltpu.make_async_remote_copy(
-                edge_scaled.at[side],
-                edge_next.at[side],
-                edge_send.at[side],
-                edge_recv.at[side],
-                device_id=(ahead, peer),
-                device_id_type=MESH,
-            )
-        )
-        sends.append(
-            pltpu.make_async_remote_copy(
-                edge_raw.at[side],
-                edge_in.at[side],
-                edge_send.at[2 + side],
-                edge_recv.at[2 + side],
-                device_id=(q, peer),
-                device_id_type=MESH,
-            )
-        )
-    for send in sends:
-        send.start()
-    main_out[...] = keep * lat_f[...] + gain * own
+    main_out[...] = keep * lat_f[...] + gain * noise
     main_send_copy = pltpu.make_async_remote_copy(
         main_out, main_in, main_send, main_recv, device_id=(ahead, s), device_id_type=MESH
     )
@@ -548,19 +539,13 @@
         for f in range(FRAMES):
             out[pl.ds(f, 12, stride=FRAMES), :] = v[0:12, f * COLS : (f + 1) * COLS]
 
-    sends[1].wait_recv()
-    sends[3].wait_recv()
-    put(noise_ref, own + jnp.where(first, 0.0, edge_in[0]) + jnp.where(last, 0.0, edge_in[1]))
+    put(noise_ref, noise)
     main_send_copy.wait_recv()
-    sends[0].wait_recv()
-    sends[2].wait_recv()
-    put(next_ref, main_in[...] + jnp.where(first, 0.0, edge_next[0]) + jnp.where(last, 0.0, edge_next[1]))
+    put(next_ref, main_in[...])
 
     pltpu.make_async_copy(lat_b.at[pl.ds(0, (ns - 1) * 16)], lat_b.at[pl.ds(0, (ns - 1) * 16)], lat_send).wait()
     for phase in range(3):
         stats_sent(phase)
-    for send in sends:
-        send.wait_send()
     main_send_copy.wait_send()
 
 
@@ -605,39 +590,33 @@
         + [
             DMA((len(operands),)),
             pltpu.VMEM((16, CELLS), F32),
-            pltpu.VMEM(((ns + 2) * 16, CELLS), BF),
-            pltpu.VMEM((3, (ns + 2) * 16, CELLS), BF),
+            pltpu.VMEM(((ns + 4) * 16, CELLS), BF),
+            pltpu.VMEM((3, (ns + 4) * 16, CELLS), BF),
             pltpu.VMEM((40, CH), F32),
             pltpu.VMEM((7, 144, CH), BF),
+            pltpu.VMEM((9 * CELLS, CH), F32),
             pltpu.VMEM((7 * CELLS, CH), F32),
             pltpu.VMEM((5 * CELLS, CH), F32),
-            pltpu.VMEM((3 * CELLS, CH), F32),
-            pltpu.VMEM((7 * CELLS, MAIN), BF),
-            pltpu.VMEM((9 * CELLS, 256), BF),
+            pltpu.VMEM((9 * CELLS, MAIN), BF),
+            pltpu.VMEM((11 * CELLS, 256), BF),
             pltpu.VMEM((2, 3, 256, MAIN), BF),
             pltpu.VMEM((2, 1024, 256), BF),
             pltpu.VMEM((CH, 1024), BF),
             pltpu.VMEM((384, CH), BF),
-            pltpu.VMEM((ROWS * CELLS, 1024), BF),
+            pltpu.VMEM(((ROWS + 2) * CELLS, 1024), BF),
             pltpu.VMEM((CH, CH), BF),
             pltpu.VMEM((1, CH), F32),
             pltpu.VMEM((40, CH), F32),
-            pltpu.VMEM((3, 144, CH), BF),
-            pltpu.VMEM((ROWS * CELLS, 384), BF),
+            pltpu.VMEM((5, 48, CH), BF),
+            pltpu.VMEM(((ROWS + 2) * CELLS, 384), BF),
             pltpu.VMEM((2, 8, CH), F32),
             pltpu.VMEM((3, ns, 2, CH), F32),
-            pltpu.VMEM((2, 16, CELLS), F32),
-            pltpu.VMEM((2, 16, CELLS), F32),
-            pltpu.VMEM((2, 16, CELLS), F32),
-            pltpu.VMEM((2, 16, CELLS), F32),
             pltpu.VMEM((16, CELLS), F32),
             pltpu.VMEM((16, CELLS), F32),
             DMA,
+            DMA((5,)),
             DMA((3,)),
             DMA((3,)),
-            DMA((3,)),
-            DMA((4,)),
-            DMA((4,)),
             DMA,
             DMA,
         ],

time: 49.2 us -> 46.9 us (0.953)
  Pallas kernels: 47 us -> 44.8 us
    pallas_call x1, Pallas kernels: 47 us -> 44.8 us  [per_device(): pl.pallas_call(functools.partial(kernel, nq, ns), out_shape=(jax.ShapeDty...]
where the time goes in v4:
time: 46.9 us; the launch traced here: 46.8 us
  Pallas kernels  44.8 us (96%)
  between operations  0.67 us (1%)
  other arithmetic  0.66 us (1%)
  local copies, waits for them, and re-layouts  0.64 us (1%)
    pallas_call x1, Pallas kernels, per_device(): pl.pallas_call(functools.partial(kernel, nq, ns), out_shape=(jax.ShapeDty...  44.8 us

profile of v4, /device:TPU:1, one launch (start us, length us, event | category | flops | bytes accessed | tf_op | source)
XLA Modules:
  0.0 46.8 jit_solution(8728055865604936730)
XLA Ops:
  0.6 0.0 copy-start
  0.7 44.8 %shard_map.140 = (f32[192,16]{1,0:T(8,128)S(1)}, f32[192,16]{1,0:T(8,128)S(1)}) custom-call(s32[16]{0:T(128)} %ts_hbm.1, s32[16]{0:T(128)} %map_hbm.1, f32[192,16]{1,0:T(8,128)} %bitcast.20, bf16[3,3,4,320]{3,2,1,0:T(4,128)(2,1)} %cin_hbm.1, bf16[320,1280]{1,0:T(8,128)(2,1)} %tw1_hbm.1, bf16[1280,1280]{1,0:T(8,128)(2,1)} %tw2_hbm.1, ...), custom_call_target="tpu_custom_call" | custom-call | flops 10000000000 | bytes 10000000 | tf_op jit(solution)/shard_map/pallas_call | solution.py:579
  45.5 0.0 copy-done
  45.5 0.7 %select_bitcast_fusion = f32[1,4,16,3,16]{4,2,3,1,0:T(8,128)} fusion(f32[4,16,3,16]{3,1,2,0:T(8,128)S(1)} %copy-done, f32[4,16,3,16]{3,1,2,0:T(8,128)S(1)} %bitcast.18, pred[]{:T(512)S(6)} %eq.3), kind=kLoop, calls=%fused_computation | loop fusion | flops 3072 | bytes 36865 | tf_op jit(solution)/shard_map/broadcast_in_dim | solution.py:633
  46.2 0.6 %copy.16 = f32[1,4,16,3,16]{4,2,3,1,0:T(8,128)} copy(f32[1,4,16,3,16]{4,2,3,1,0:T(8,128)S(1)} %bitcast.17) | data formatting | bytes 24576
Async XLA Ops:
  0.6 44.9 %copy-start = (f32[4,16,3,16]{3,1,2,0:T(8,128)S(1)}, f32[4,16,3,16]{3,1,2,0:T(8,128)}, u32[]{:S(2)}) copy-start(f32[4,16,3,16]{3,1,2,0:T(8,128)} %param.14) | copy-start | bytes 36868

commit v5 on v4

--- a/solution.py
+++ b/solution.py
@@ -95,6 +95,8 @@
     block,
     xm,
     xr,
+    xm2,
+    xr2,
     kr,
     nr,
     wqkv,
@@ -128,12 +130,8 @@
 
     barrier = pltpu.get_barrier_semaphore()
 
-    def greet(j, _):
-        peer = lax.rem(s + j, ns)
-        pl.semaphore_signal(barrier, inc=1, device_id=(q, peer), device_id_type=MESH)
-        return 0
-
-    lax.fori_loop(1, ns, greet, 0)
+    for j in order:
+        pl.semaphore_signal(barrier, inc=1, device_id=(q, lax.rem(s + j, ns)), device_id_type=MESH)
     pl.semaphore_signal(barrier, inc=1, device_id=(behind, s), device_id_type=MESH)
 
     loads = [
@@ -142,22 +140,22 @@
             (
                 (lat_hbm, lat_v),
                 (cin_hbm, cin_v),
+                (c1_hbm, c1_v),
+                (ts_hbm, ts_ref),
+                (map_hbm, map_ref),
                 (tw1_hbm, tw1_v),
                 (tw2_hbm, tw2_v),
                 (emb_hbm, emb_v),
-                (c1_hbm, c1_v),
                 (c2_hbm, c2_v),
                 (qkv_hbm, qkv_v),
                 (proj_hbm, proj_v),
                 (cout_hbm, cout_v),
-                (ts_hbm, ts_ref),
-                (map_hbm, map_ref),
             )
         )
     ]
     for load in loads:
         load.start()
-    load_lat, load_cin, load_tw1, load_tw2, load_emb, load_c1, load_c2, load_qkv, load_proj, load_cout, load_ts, load_map = loads
+    load_lat, load_cin, load_c1, load_ts, load_map, load_tw1, load_tw2, load_emb, load_c2, load_qkv, load_proj, load_cout = loads
 
     load_lat.wait()
     lat_f[12:16, :] = jnp.where(iota((4, CELLS), 0) == 0, 1.0, 0.0)
@@ -184,22 +182,6 @@
     for j in order:
         lat_sends[j].start()
 
-    load_ts.wait()
-    load_map.wait()
-    level = ts_ref[map_ref[q]]
-    pos = iota((16, CH), 1)
-    half = CH // 2
-    k = jnp.where(pos < half, pos, pos - half).astype(F32)
-    phases = level.astype(F32) * jnp.exp(k * (-math.log(10000.0) / half))
-    sinusoid = jnp.where(pos < half, jnp.cos(phases), jnp.sin(phases)).astype(BF)
-    load_tw1.wait()
-    h = dot(sinusoid, tw1_v[...])
-    first_hidden = silu_of_half(0.5 * h).astype(BF)
-    load_tw2.wait()
-    h = dot(first_hidden, tw2_v[...])
-    second = silu_of_half(0.5 * h).astype(BF)
-    load_emb.wait()
-    bias[...] = dot_nt(second, emb_v[...])[0:1]
     ci = iota((CH, CH), 0) * 6554 >> 16
     cj = iota((CH, CH), 1) * 6554 >> 16
     pairs[...] = jnp.where(ci == cj, 1.0, 0.0).astype(BF)
@@ -219,16 +201,14 @@
     chan = in_block * 21846 >> 16
     row_of = 3 * (left >> 4) + in_block - 3 * chan
 
-    def place_cin(y, _):
+    for y in range(7):
         tap_a = row_of - y
         hit = (tap_a >= 0) & (tap_a < 3) & (in_block < 12) & (jj == (tap_a * 3 + tap_b) * 4 + chan)
         sel = jnp.where(hit, 1.0, 0.0).astype(BF)
         cin_w[y] = dot(sel, cin_f[...].astype(BF)).astype(BF)
-        return 0
-
-    lax.fori_loop(0, 7, place_cin, 0)
 
     xr[:, 192:256] = jnp.zeros((11 * CELLS, 64), BF)
+    xr2[:, 192:256] = jnp.zeros((9 * CELLS, 64), BF)
 
     def shared_passes(which, w):
         for b in range(3):
@@ -310,25 +290,29 @@
             stats.at[phase, pl.ds(0, ns - 1)], stats.at[phase, pl.ds(0, ns - 1)], stat_send.at[phase]
         ).wait()
 
-    def put_normed(r, y):
+    inputs = ((xm, xr), (xm2, xr2))
+
+    def put_normed(which, r, y):
         yb = y.astype(BF)
-        xm[cells(r), :] = yb[:, 0:MAIN]
+        alone, shared = inputs[which]
+        alone[cells(r), :] = yb[:, 0:MAIN]
         rest = yb[:, MAIN:CH]
-        xr[cells(r + 2), 0:REST] = rest
-        xr[cells(r + 1), REST : 2 * REST] = rest
-        xr[cells(r), 2 * REST : 3 * REST] = rest
+        shared[cells(r + 2), 0:REST] = rest
+        shared[cells(r + 1), REST : 2 * REST] = rest
+        shared[cells(r), 2 * REST : 3 * REST] = rest
 
     def column(n, width, x):
         return jnp.where((iota((n * CELLS, width), 0) & (COLS - 1)) == x, 0.0, 1.0)
 
     def conv_rows(which, w, rows):
+        alone, shared = inputs[which]
         n = len(rows)
         size = n * CELLS
 
         def window(ref, a):
             return jnp.concatenate([ref[cells(y + a), :] for y in rows], axis=0)
 
-        x = jnp.concatenate([window(xm, 0), window(xm, 1), window(xm, 2), window(xr, 2)], axis=1)
+        x = jnp.concatenate([window(alone, 0), window(alone, 1), window(alone, 2), window(shared, 2)], axis=1)
         z = [
             dot(
                 x,
@@ -373,15 +357,15 @@
     inv = lax.rsqrt(jnp.maximum(spread, 0.0) + NORM_EPS)
     half_inv = 0.5 * inv
 
-    def normed(r, x, mean, half_inv, row):
+    def normed(which, r, x, mean, half_inv, row):
         inside = jnp.where((s * ROWS + row >= 0) & (s * ROWS + row < ns * ROWS), half_inv, 0.0)
-        put_normed(r, silu_of_half((x - mean) * inside))
-
-    def norm1(r, _):
-        normed(r, stream[cells(r), :], mean, half_inv, r - 3)
-        return 0
-
-    lax.fori_loop(2, 7, norm1, 0)
+        put_normed(which, r, silu_of_half((x - mean) * inside))
+
+    def norm1(r):
+        normed(0, r, stream[cells(r), :], mean, half_inv, r - 3)
+
+    for r in range(2, 7):
+        norm1(r)
 
     def hidden_rows(rows):
         main, rest = conv_rows(0, c1_v, rows)
@@ -394,9 +378,26 @@
         row_stats(i, hidden[cells(i + 2), :])
     near2 = send_stats(0)
 
-    lax.fori_loop(0, 2, norm1, 0)
-    lax.fori_loop(7, 9, norm1, 0)
-    hidden_rows((0, 1, 5, 6))
+    norm1(1)
+    norm1(7)
+    hidden_rows((1, 5))
+
+    load_ts.wait()
+    load_map.wait()
+    level = ts_ref[map_ref[q]]
+    pos = iota((16, CH), 1)
+    half = CH // 2
+    k = jnp.where(pos < half, pos, pos - half).astype(F32)
+    phases = level.astype(F32) * jnp.exp(k * (-math.log(10000.0) / half))
+    sinusoid = jnp.where(pos < half, jnp.cos(phases), jnp.sin(phases)).astype(BF)
+    load_tw1.wait()
+    h = dot(sinusoid, tw1_v[...])
+    first_hidden = silu_of_half(0.5 * h).astype(BF)
+    load_tw2.wait()
+    h = dot(first_hidden, tw2_v[...])
+    second = silu_of_half(0.5 * h).astype(BF)
+    load_emb.wait()
+    bias[...] = dot_nt(second, emb_v[...])[0:1]
     load_c2.wait()
     shared_passes(1, c2_v)
 
@@ -404,11 +405,11 @@
     mean2 = mean2 - bias[...]
     half_inv2 = 0.5 * inv2
 
-    def norm2(r, _):
-        normed(r, hidden[cells(r), :], mean2, half_inv2, r - 2)
-        return 0
-
-    lax.fori_loop(1, 6, norm2, 0)
+    def norm2(r):
+        normed(1, r, hidden[cells(r), :], mean2, half_inv2, r - 2)
+
+    for r in range(1, 6):
+        norm2(r)
 
     def block_rows(rows):
         main, rest = conv_rows(1, c2_v, rows)
@@ -421,8 +422,11 @@
         row_stats(i, block[cells(i + 1), :])
     near3 = send_stats(1)
 
-    norm2(0, 0)
-    norm2(6, 0)
+    norm1(0)
+    norm1(8)
+    hidden_rows((0, 6))
+    norm2(0)
+    norm2(6)
     block_rows((0, 4))
 
     load_qkv.wait()
@@ -479,7 +483,7 @@
     own_cells = cells(1, ROWS)
     project(own_cells)
 
-    def attend_row(i, _):
+    def attend_row(i):
         row = cells(i)
         ones = jnp.ones((CELLS, 128), BF)
 
@@ -497,9 +501,9 @@
         attended[row, 0:128] = jnp.where(low_half, 0.0, head(0)).astype(BF)
         attended[row, 128:256] = jnp.where(low_half, head(1), head(2)).astype(BF)
         attended[row, 256:384] = jnp.where(low_half, head(3), head(4)).astype(BF)
-        return 0
-
-    lax.fori_loop(1, ROWS + 1, attend_row, 0)
+
+    for i in range(1, ROWS + 1):
+        attend_row(i)
     mix(own_cells)
     for i in range(ROWS):
         row_stats(i, block[cells(i + 1), :])
@@ -508,10 +512,8 @@
     for i in (0, ROWS + 1):
         project(cells(i))
 
-    def attend_halo(i, _):
-        return attend_row(i * (ROWS + 1), 0)
-
-    lax.fori_loop(0, 2, attend_halo, 0)
+    for i in (0, ROWS + 1):
+        attend_row(i)
     for i in (0, ROWS + 1):
         mix(cells(i))
 
@@ -599,6 +601,8 @@
             pltpu.VMEM((5 * CELLS, CH), F32),
             pltpu.VMEM((9 * CELLS, MAIN), BF),
             pltpu.VMEM((11 * CELLS, 256), BF),
+            pltpu.VMEM((7 * CELLS, MAIN), BF),
+            pltpu.VMEM((9 * CELLS, 256), BF),
             pltpu.VMEM((2, 3, 256, MAIN), BF),
             pltpu.VMEM((2, 1024, 256), BF),
             pltpu.VMEM((CH, 1024), BF),

time: 46.9 us -> 44.4 us (0.947)
  Pallas kernels: 44.8 us -> 42.4 us
    pallas_call x1, Pallas kernels: 44.8 us -> 42.4 us  [per_device(): pl.pallas_call(functools.partial(kernel, nq, ns), out_shape=(jax.ShapeDty...]
where the time goes in v5:
time: 44.4 us
  Pallas kernels  42.4 us (95%)
  between operations  0.67 us (2%)
  other arithmetic  0.66 us (1%)
  local copies, waits for them, and re-layouts  0.64 us (1%)
    pallas_call x1, Pallas kernels, per_device(): pl.pallas_call(functools.partial(kernel, nq, ns), out_shape=(jax.ShapeDty...  42.4 us

profile of v5, /device:TPU:1, one launch (start us, length us, event | category | flops | bytes accessed | tf_op | source)
XLA Modules:
  0.0 44.4 jit_solution(5232568243827894267)
XLA Ops:
  0.6 0.0 copy-start
  0.7 42.4 %shard_map.140 = (f32[192,16]{1,0:T(8,128)S(1)}, f32[192,16]{1,0:T(8,128)S(1)}) custom-call(s32[16]{0:T(128)} %ts_hbm.1, s32[16]{0:T(128)} %map_hbm.1, f32[192,16]{1,0:T(8,128)} %bitcast.20, bf16[3,3,4,320]{3,2,1,0:T(4,128)(2,1)} %cin_hbm.1, bf16[320,1280]{1,0:T(8,128)(2,1)} %tw1_hbm.1, bf16[1280,1280]{1,0:T(8,128)(2,1)} %tw2_hbm.1, ...), custom_call_target="tpu_custom_call" | custom-call | flops 10000000000 | bytes 10000000 | tf_op jit(solution)/shard_map/pallas_call | solution.py:581
  43.0 0.0 copy-done
  43.1 0.7 %select_bitcast_fusion = f32[1,4,16,3,16]{4,2,3,1,0:T(8,128)} fusion(f32[4,16,3,16]{3,1,2,0:T(8,128)S(1)} %copy-done, f32[4,16,3,16]{3,1,2,0:T(8,128)S(1)} %bitcast.18, pred[]{:T(512)S(6)} %eq.3), kind=kLoop, calls=%fused_computation | loop fusion | flops 3072 | bytes 36865 | tf_op jit(solution)/shard_map/broadcast_in_dim | solution.py:637
  43.7 0.6 %copy.16 = f32[1,4,16,3,16]{4,2,3,1,0:T(8,128)} copy(f32[1,4,16,3,16]{4,2,3,1,0:T(8,128)S(1)} %bitcast.17) | data formatting | bytes 24576
Async XLA Ops:
  0.6 42.4 %copy-start = (f32[4,16,3,16]{3,1,2,0:T(8,128)S(1)}, f32[4,16,3,16]{3,1,2,0:T(8,128)}, u32[]{:S(2)}) copy-start(f32[4,16,3,16]{3,1,2,0:T(8,128)} %param.14) | copy-start | bytes 36868

commit v6 on v5

--- a/solution.py
+++ b/solution.py
@@ -232,6 +232,8 @@
         shifted[1, rows, :] = lat_b[rows, :]
         shifted[2, rows, :] = jnp.where(lane == COLS - 1, 0.0, pltpu.roll(v, CELLS - 1, 1)).astype(BF)
 
+    load_c1.wait()
+    shared_passes(0, c1_v)
     for j in (1, 2, ns - 2, ns - 1):
         lat_sends[j].wait_recv()
     shift_blocks(s, 5)
@@ -241,10 +243,8 @@
         return jnp.concatenate([shifted[b, window, :] for b in range(3)], axis=0).astype(F32).T.astype(BF)
 
     x_in = cells_of(s + 1)
-    for y in range(7):
+    for y in range(1, 6):
         stream[cells(y + 1), :] = dot(x_in, cin_w[y])
-    stream[cells(0), :] = dot(cells_of(s), cin_w[2])
-    stream[cells(8), :] = dot(cells_of(s + 2), cin_w[4])
 
     def row_stats(r, x):
         m = jnp.sum(x, axis=0, keepdims=True) * (1.0 / CELLS)
@@ -333,8 +333,6 @@
         )
         return main, rest
 
-    load_c1.wait()
-    shared_passes(0, c1_v)
 
     pltpu.make_async_copy(lat_b.at[pl.ds(0, (ns - 5) * 16)], lat_b.at[pl.ds(0, (ns - 5) * 16)], lat_recv.at[4]).wait()
     shift_blocks(1, ns + 2)
@@ -378,6 +376,9 @@
         row_stats(i, hidden[cells(i + 2), :])
     near2 = send_stats(0)
 
+    x_in = cells_of(s + 1)
+    stream[cells(1), :] = dot(x_in, cin_w[0])
+    stream[cells(7), :] = dot(x_in, cin_w[6])
     norm1(1)
     norm1(7)
     hidden_rows((1, 5))
@@ -400,35 +401,6 @@
     bias[...] = dot_nt(second, emb_v[...])[0:1]
     load_c2.wait()
     shared_passes(1, c2_v)
-
-    mean2, inv2 = take_stats(0, near2, bias[...])
-    mean2 = mean2 - bias[...]
-    half_inv2 = 0.5 * inv2
-
-    def norm2(r):
-        normed(1, r, hidden[cells(r), :], mean2, half_inv2, r - 2)
-
-    for r in range(1, 6):
-        norm2(r)
-
-    def block_rows(rows):
-        main, rest = conv_rows(1, c2_v, rows)
-        for i, j in enumerate(rows):
-            block[cells(j), 0:MAIN] = stream[cells(j + 2), 0:MAIN] + main[i * CELLS : (i + 1) * CELLS]
-            block[cells(j), MAIN:CH] = stream[cells(j + 2), MAIN:CH] + rest[i * CELLS : (i + 1) * CELLS]
-
-    block_rows((1, 2, 3))
-    for i in range(ROWS):
-        row_stats(i, block[cells(i + 1), :])
-    near3 = send_stats(1)
-
-    norm1(0)
-    norm1(8)
-    hidden_rows((0, 6))
-    norm2(0)
-    norm2(6)
-    block_rows((0, 4))
-
     load_qkv.wait()
     wqkv[:, 0:CH] = qkv_v[:, 0:CH] * jnp.asarray(HEAD_DIM**-0.5, BF)
     wqkv[:, CH:384] = jnp.zeros((CH, 384 - CH), BF)
@@ -436,6 +408,85 @@
     load_proj.wait()
     wproj[0:64, :] = jnp.zeros((64, CH), BF)
     wproj[64:384, :] = proj_v[...]
+
+    mean2, inv2 = take_stats(0, near2, bias[...])
+    mean2 = mean2 - bias[...]
+    half_inv2 = 0.5 * inv2
+
+    def norm2(r):
+        normed(1, r, hidden[cells(r), :], mean2, half_inv2, r - 2)
+
+    for r in range(1, 6):
+        norm2(r)
+
+    def block_rows(rows):
+        main, rest = conv_rows(1, c2_v, rows)
+        for i, j in enumerate(rows):
+            block[cells(j), 0:MAIN] = stream[cells(j + 2), 0:MAIN] + main[i * CELLS : (i + 1) * CELLS]
+            block[cells(j), MAIN:CH] = stream[cells(j + 2), MAIN:CH] + rest[i * CELLS : (i + 1) * CELLS]
+
+    block_rows((1, 2, 3))
+    for i in range(ROWS):
+        row_stats(i, block[cells(i + 1), :])
+    near3 = send_stats(1)
+
+    stream[cells(0), :] = dot(cells_of(s), cin_w[2])
+    stream[cells(8), :] = dot(cells_of(s + 2), cin_w[4])
+    norm1(0)
+    norm1(8)
+    hidden_rows((0, 6))
+    norm2(0)
+    norm2(6)
+    block_rows((0, 4))
+
+    mean3, inv3 = take_stats(1, near3)
+
+    same = ((iota((CELLS, CELLS), 0) ^ iota((CELLS, CELLS), 1)) & (COLS - 1)) == 0
+    low_half = iota((CELLS, 128), 1) < HEAD_DIM
+
+    def project(rows):
+        projected[rows, :] = dot(((block[rows, :] - mean3) * inv3).astype(BF), wqkv[...]).astype(BF)
+
+    def mix(rows):
+        block[rows, :] += dot(attended[rows, :], wproj[...])
+
+    own_cells = cells(1, ROWS)
+    project(own_cells)
+
+    def attend_row(i):
+        row = cells(i)
+        ones = jnp.ones((CELLS, 128), BF)
+
+        def head(h):
+            qt = projected[row, h // 2 * 128 : h // 2 * 128 + 128]
+            if h < HEADS - 1:
+                qt = jnp.where(low_half if h % 2 == 0 else jnp.logical_not(low_half), qt, jnp.zeros_like(qt))
+            kt = projected[row, 384 + h // 2 * 128 : 512 + h // 2 * 128]
+            vt = projected[row, 640 + (h + 1) // 2 * 128 : 768 + (h + 1) // 2 * 128]
+            sc = jnp.where(same, dot_nt(qt, kt), -1e30)
+            p = jnp.exp(sc - jnp.max(sc, axis=1, keepdims=True)).astype(BF)
+            o = dot(p, jnp.concatenate([vt, ones], axis=1))
+            return o[:, 0:128] / o[:, 128:256]
+
+        attended[row, 0:128] = jnp.where(low_half, 0.0, head(0)).astype(BF)
+        attended[row, 128:256] = jnp.where(low_half, head(1), head(2)).astype(BF)
+        attended[row, 256:384] = jnp.where(low_half, head(3), head(4)).astype(BF)
+
+    for i in range(1, ROWS + 1):
+        attend_row(i)
+    mix(own_cells)
+    for i in range(ROWS):
+        row_stats(i, block[cells(i + 1), :])
+    near4 = send_stats(2)
+
+    for i in (0, ROWS + 1):
+        project(cells(i))
+
+    for i in (0, ROWS + 1):
+        attend_row(i)
+    for i in (0, ROWS + 1):
+        mix(cells(i))
+
     load_cout.wait()
     cout_f[36:40, :] = jnp.zeros((4, CH), F32)
     for a in range(3):
@@ -468,54 +519,6 @@
     alpha_next = alpha(level - STEP)
     keep = jnp.sqrt(alpha_next / alpha_now)
     gain = jnp.sqrt(1.0 - alpha_next) - keep * jnp.sqrt(1.0 - alpha_now)
-
-    mean3, inv3 = take_stats(1, near3)
-
-    same = ((iota((CELLS, CELLS), 0) ^ iota((CELLS, CELLS), 1)) & (COLS - 1)) == 0
-    low_half = iota((CELLS, 128), 1) < HEAD_DIM
-
-    def project(rows):
-        projected[rows, :] = dot(((block[rows, :] - mean3) * inv3).astype(BF), wqkv[...]).astype(BF)
-
-    def mix(rows):
-        block[rows, :] += dot(attended[rows, :], wproj[...])
-
-    own_cells = cells(1, ROWS)
-    project(own_cells)
-
-    def attend_row(i):
-        row = cells(i)
-        ones = jnp.ones((CELLS, 128), BF)
-
-        def head(h):
-            qt = projected[row, h // 2 * 128 : h // 2 * 128 + 128]
-            if h < HEADS - 1:
-                qt = jnp.where(low_half if h % 2 == 0 else jnp.logical_not(low_half), qt, jnp.zeros_like(qt))
-            kt = projected[row, 384 + h // 2 * 128 : 512 + h // 2 * 128]
-            vt = projected[row, 640 + (h + 1) // 2 * 128 : 768 + (h + 1) // 2 * 128]
-            sc = jnp.where(same, dot_nt(qt, kt), -1e30)
-            p = jnp.exp(sc - jnp.max(sc, axis=1, keepdims=True)).astype(BF)
-            o = dot(p, jnp.concatenate([vt, ones], axis=1))
-            return o[:, 0:128] / o[:, 128:256]
-
-        attended[row, 0:128] = jnp.where(low_half, 0.0, head(0)).astype(BF)
-        attended[row, 128:256] = jnp.where(low_half, head(1), head(2)).astype(BF)
-        attended[row, 256:384] = jnp.where(low_half, head(3), head(4)).astype(BF)
-
-    for i in range(1, ROWS + 1):
-        attend_row(i)
-    mix(own_cells)
-    for i in range(ROWS):
-        row_stats(i, block[cells(i + 1), :])
-    near4 = send_stats(2)
-
-    for i in (0, ROWS + 1):
-        project(cells(i))
-
-    for i in (0, ROWS + 1):
-        attend_row(i)
-    for i in (0, ROWS + 1):
-        mix(cells(i))
 
     mean4, inv4 = take_stats(2, near4)
     half_inv4 = 0.5 * inv4

time: 44.4 us -> 44.2 us (level)
  no operation moved by 1% of the time
where the time goes in v6:
time: 44.2 us; the launch traced here: 44.1 us
  Pallas kernels  42.2 us (95%)
  between operations  0.67 us (2%)
  other arithmetic  0.66 us (1%)
  local copies, waits for them, and re-layouts  0.64 us (1%)
    pallas_call x1, Pallas kernels, per_device(): pl.pallas_call(functools.partial(kernel, nq, ns), out_shape=(jax.ShapeDty...  42.2 us

profile of v6, /device:TPU:1, one launch (start us, length us, event | category | flops | bytes accessed | tf_op | source)
XLA Modules:
  0.0 44.1 jit_solution(686502708524127408)
XLA Ops:
  0.6 0.0 copy-start
  0.7 42.2 %shard_map.140 = (f32[192,16]{1,0:T(8,128)S(1)}, f32[192,16]{1,0:T(8,128)S(1)}) custom-call(s32[16]{0:T(128)} %ts_hbm.1, s32[16]{0:T(128)} %map_hbm.1, f32[192,16]{1,0:T(8,128)} %bitcast.20, bf16[3,3,4,320]{3,2,1,0:T(4,128)(2,1)} %cin_hbm.1, bf16[320,1280]{1,0:T(8,128)(2,1)} %tw1_hbm.1, bf16[1280,1280]{1,0:T(8,128)(2,1)} %tw2_hbm.1, ...), custom_call_target="tpu_custom_call" | custom-call | flops 10000000000 | bytes 10000000 | tf_op jit(solution)/shard_map/pallas_call | solution.py:584
  42.8 0.0 copy-done
  42.8 0.7 %select_bitcast_fusion = f32[1,4,16,3,16]{4,2,3,1,0:T(8,128)} fusion(f32[4,16,3,16]{3,1,2,0:T(8,128)S(1)} %copy-done, f32[4,16,3,16]{3,1,2,0:T(8,128)S(1)} %bitcast.18, pred[]{:T(512)S(6)} %eq.3), kind=kLoop, calls=%fused_computation | loop fusion | flops 3072 | bytes 36865 | tf_op jit(solution)/shard_map/broadcast_in_dim | solution.py:640
  43.5 0.6 %copy.16 = f32[1,4,16,3,16]{4,2,3,1,0:T(8,128)} copy(f32[1,4,16,3,16]{4,2,3,1,0:T(8,128)S(1)} %bitcast.17) | data formatting | bytes 24576
Async XLA Ops:
  0.6 42.2 %copy-start = (f32[4,16,3,16]{3,1,2,0:T(8,128)S(1)}, f32[4,16,3,16]{3,1,2,0:T(8,128)}, u32[]{:S(2)}) copy-start(f32[4,16,3,16]{3,1,2,0:T(8,128)} %param.14) | copy-start | bytes 36868
